TPU v7x, 256 devices: a whole 4x4x8 slice. The times are simulated.
256 devices in a mesh: wire: 128 (over x, z_hi, y, core), col: 2 (over z_lo).
Axes of the slice: x: 4, y: 4, z: 8 (z_hi: 4, z_lo: 2; z = z_hi * 2 + z_lo), core: 2. Of those that a mesh axis runs over, the one named last changes fastest.
Arguments:
- hamiltonian: bfloat16 [2048, 3, 128, 128], P('wire')
- offsets: int32 [2048, 3], P('wire'), may hold values from -2 to 2, as said below
- phase_left: bfloat16 [262144, 2048], P('wire'), may hold values from -0.125 to 0.125
- phase_right: bfloat16 [262144, 2048], P('wire'), may hold values from -0.01171875 to 0.01171875
- orbitals: bfloat16 [262144, 512], P('wire', 'col'), may hold values from -6 to 6
Outputs:
- gradient: float32 [262144, 512], P('wire', 'col')
Inputs may be any that keep to these rules, and one draw needn't show every extreme that they name: `offsets`: slot 0 of every row block has offset 0.
All inputs are finite; a program needn't handle non-finite values.
Results may differ from a plain program's by a relative error of at most 0.0017.
Values may be sent and summed in bfloat16 or wider, within the bound.
A program may use at most 128 MiB of HBM per device.

v0:
```python
import jax
import jax.numpy as jnp
from jax import lax
from jax.sharding import Mesh
from jax.sharding import PartitionSpec as P

REACH = 2
WIRE = ("wire_0", "wire_1", "wire_2", "wire_3")


def padded_2(shard, sides, width):
    for axis, dim in sides:
        devices, length = (lax.axis_size(axis), shard.shape[dim])
        up = [(i, (i + 1) % devices) for i in range(devices)]
        down = [(j, i) for i, j in up]
        last = lax.slice_in_dim(shard, length - width, length, axis=dim)
        leading = lax.slice_in_dim(shard, 0, width, axis=dim)
        before = lax.ppermute(last, axis, up)
        after = lax.ppermute(leading, axis, down)
        shard = jnp.concatenate([before, shard, after], axis=dim)
    return shard


def in_order(pieces, dim):
    lengths = list(pieces.shape[1:])
    lengths[dim] *= pieces.shape[0]
    return jnp.moveaxis(pieces, 0, dim).reshape(lengths)


def sent_to_all(shard, axis):
    devices = lax.axis_size(axis)
    return lax.all_to_all(
        jnp.broadcast_to(shard[None], (devices, *shard.shape)), axis, 0, 0, tiled=True
    )


def gathered_copies(shard, axis, dim):
    return in_order(sent_to_all(shard, axis), dim)


def rows_for(lines, devices):
    spare = -lines.shape[0] % devices
    if not spare:
        return lines
    return jnp.concatenate([lines, jnp.zeros((spare, *lines.shape[1:]), lines.dtype)])


def gathered_by_axis(shard, axes, dim):
    far, near = axes
    leading = sent_to_all(shard, far)
    pieces = jnp.swapaxes(sent_to_all(leading, near), 0, 1)
    return in_order(pieces.reshape(-1, *shard.shape), dim)


def in_blocks(shard, dim, devices):
    lengths = shard.shape
    pieces = shard.reshape(*lengths[:dim], devices, lengths[dim] // devices, *lengths[dim + 1 :])
    return jnp.moveaxis(pieces, dim, 0)


def summed_on_arrival(shard, axis, dim):
    pieces = in_blocks(shard, dim, lax.axis_size(axis))
    arrived = lax.all_to_all(pieces, axis, split_axis=0, concat_axis=0, tiled=True)
    return arrived.sum(axis=0)


def summed_rows(shard, axes, dim):
    far, near = axes
    pieces = in_blocks(shard, dim, lax.axis_size(far))
    nearer = summed_on_arrival(pieces, near, dim + 1)
    arrived = lax.all_to_all(nearer, far, split_axis=0, concat_axis=0, tiled=True)
    return arrived.sum(axis=0)


def sum_by_parts(shard, axes):
    padded = rows_for(shard, lax.axis_size(axes[0]) * lax.axis_size(axes[1]))
    whole = gathered_by_axis(summed_rows(padded, axes, 0), axes, 0)
    return lax.slice_in_dim(whole, 0, len(shard)).reshape(shard.shape)


def packed_total(arrays, axis):
    line, at, finished = (jnp.concatenate([a.reshape(-1) for a in arrays]), 0, [])
    running = sum_by_parts(line, axis)
    for a in arrays:
        finished.append(running[at : at + a.size].reshape(a.shape))
        at += a.size
    return tuple(finished)


def nested_sum(shard, axes):
    lines = shard.reshape(-1, shard.shape[-1])
    own = summed_rows(rows_for(lines, lax.axis_size(axes[0]) * lax.axis_size(axes[1])), axes, 0)
    whole = gathered_by_axis(own, axes, 0)
    return whole[: len(lines)].reshape(shard.shape)


def body(hamiltonian, offsets, phase_left, phase_right, orbitals):
    local_blocks = hamiltonian.shape[0]
    block_size = hamiltonian.shape[2]
    local_rows = orbitals.shape[0]
    total_rows = local_rows * lax.axis_size(WIRE)
    padded = padded_2(orbitals, ((WIRE, 0),), REACH * block_size)
    tiles = padded.reshape(local_blocks + 2 * REACH, block_size, orbitals.shape[1])
    picks = jnp.arange(local_blocks, dtype=jnp.int32)[:, None] + offsets + REACH
    picked = jnp.take(tiles, picks, axis=0)
    band = jnp.einsum(
        "jsab,jsbm->jam", hamiltonian, picked, preferred_element_type=jnp.float32
    ).reshape(local_rows, orbitals.shape[1])
    full = gathered_copies(orbitals, "col", 1)
    coupling_part = jnp.dot(phase_right.T, orbitals, preferred_element_type=jnp.float32)
    intersection_part = jnp.dot(full.T, orbitals, preferred_element_type=jnp.float32)
    coupling, intersection = packed_total(
        (coupling_part, intersection_part), (("wire_0", "wire_1", "wire_2"), "wire_3")
    )
    coupling_low = coupling.astype(jnp.bfloat16)
    image = band + jnp.dot(phase_left, coupling_low, preferred_element_type=jnp.float32)
    full_wide = full.astype(jnp.float32)
    cross_part = jnp.dot(full_wide.T, image, precision=lax.Precision.HIGHEST)
    cross = nested_sum(cross_part, (("wire_0", "wire_1", "wire_2"), "wire_3"))
    intersection_scaled = intersection / total_rows
    cross_scaled = cross / total_rows
    partial_terms = jnp.dot(image, intersection_scaled.T, precision=lax.Precision.HIGHEST)
    mixed = summed_on_arrival(partial_terms, "col", 1)
    gradient = (
        2.0 * image - mixed - jnp.dot(full_wide, cross_scaled, precision=lax.Precision.HIGHEST)
    )
    return gradient


def solution(mesh):
    finer = Mesh(
        mesh.devices.reshape(4, 4, 4, 2, mesh.shape["col"]),
        ("wire_0", "wire_1", "wire_2", "wire_3", "col"),
    )
    in_specs = (
        P(WIRE, None, None, None),
        P(WIRE, None),
        P(WIRE, None),
        P(WIRE, None),
        P(WIRE, "col"),
    )
    out_specs = P(WIRE, "col")
    return jax.shard_map(body, mesh=finer, in_specs=in_specs, out_specs=out_specs, check_vma=False)
```

profile of v0, /device:TPU:1, one launch (start us, length us, event | category | flops | bytes accessed | tf_op | source)
XLA Modules:
  0.0 309.7 jit_solution(2495523593434525843)
XLA Ops:
  0.0 1.6 copy.54
  1.6 1.6 broadcast_in_dim.48
  3.2 4.9 %all-to-all-start = ((bf16[2,2048,256]{1,2,0:T(8,128)(2,1)}), bf16[2,2048,256]{1,2,0:T(8,128)(2,1)}, u32[]{:S(2)}, u32[]{:S(2)}) async-start(bf16[2,2048,256]{1,2,0:T(8,128)(2,1)} %broadcast_in_dim.48), calls=%async_computation | async-start | bytes 4194304 | tf_op jit(solution)/shard_map/all_to_all | solution.py:32
  8.1 5.9 %convolution_bitcast_fusion.3 = f32[256,2,8,128]{3,2,1,0:T(8,128)S(1)} fusion(bf16[2048,2048]{1,0:T(8,128)(2,1)} %param.8, bf16[2048,256]{1,0:T(8,128)(2,1)S(1)} %copy-done.4), kind=kOutput, calls=%fused_computation.12 | convolution fusion | flops 2147483648 | bytes 11534336 | tf_op jit(solution)/shard_map/dot_general | solution.py:110
  14.0 2.4 copy.70
  16.4 15.6 %all-to-all-done = bf16[2,2048,256]{1,2,0:T(8,128)(2,1)} async-done(((bf16[2,2048,256]{1,2,0:T(8,128)(2,1)}), bf16[2,2048,256]{1,2,0:T(8,128)(2,1)}, u32[]{:S(2)}, u32[]{:S(2)}) %all-to-all-start) | async-done | bytes 2097184 | tf_op jit(solution)/shard_map/all_to_all | solution.py:32
  32.0 2.4 convolution_bitcast_fusion.5
  34.4 0.3 copy.71
  34.7 1.7 pad_maximum_fusion
  36.4 4.3 %reshape_reshape.8 = f32[64,2,5120]{2,1,0:T(2,128)} reshape(f32[655360]{0:T(1024)} %pad_maximum_fusion) | data formatting | bytes 5242880 | tf_op jit(solution)/shard_map/reshape;reshape | solution.py:57
  40.7 2.6 copy.55
  43.3 9.5 %all_to_all.55 = f32[2,64,5120]{2,1,0:T(8,128)} all-to-all(f32[2,64,5120]{2,1,0:T(8,128)S(1)} %copy.55), channel_id=1, replica_groups=mesh['wire_0'=4,'wire_1'=4,'wire_2'=4,'wire_3'=2,'col'=2] {'wire_3'}, dimensions={0} | all-to-all | bytes 5242880 | tf_op jit(solution)/shard_map/all_to_all | solution.py:63
  52.8 3.1 reduce_sum.45
  55.9 2.2 all_to_all.36
  58.1 49.4 %all_to_all.56 = f32[64,1,5120]{2,1,0:T(1,128)} all-to-all(f32[64,1,5120]{2,1,0:T(1,128)S(1)} %all_to_all.36), channel_id=1, replica_groups=mesh['wire_0'=4,'wire_1'=4,'wire_2'=4,'wire_3'=2,'col'=2] {'wire_0','wir..., dimensions={0} | all-to-all | bytes 2621440 | tf_op jit(solution)/shard_map/all_to_all | solution.py:71
  107.5 2.1 reduce_sum.46
  109.6 1.8 broadcast_in_dim.49
  111.4 7.1 %all-to-all-start.3 = ((f32[64,1,5120]{2,1,0:T(1,128)}), f32[64,1,5120]{2,1,0:T(1,128)}, u32[]{:S(2)}, u32[]{:S(2)}) async-start(f32[64,1,5120]{2,1,0:T(1,128)} %broadcast_in_dim.49), calls=%async_computation.3 | async-start | bytes 2621440 | tf_op jit(solution)/shard_map/all_to_all | solution.py:32
  118.5 2.4 collective-permute-start
  121.2 3.8 %collective-permute-done = bf16[256,256]{1,0:T(8,128)(2,1)S(1)} collective-permute-done((bf16[256,256]{1,0:T(8,128)(2,1)S(1)}, bf16[256,256]{1,0:T(8,128)(2,1)S(1)}, u32[]{:S(2)}, u32[]{:S(2)}) %collective-permute-start) | collective-permute-done | bytes 131104 | tf_op jit(solution)/shard_map/ppermute | solution.py:18
  125.0 2.4 collective-permute-done.1
  127.4 1.3 pad_maximum_fusion.1
  128.7 2.6 gather_fusion
  131.3 4.0 %fusion = f32[16,256,128,1]{1,2,3,0:T(8,128)} fusion(bf16[16,3,128,128]{3,2,1,0:T(8,128)(2,1)S(1)} %copy-done, bf16[16,3,128,256]{3,2,1,0:T(8,128)(2,1)} %bitcast.57, pred[16,3]{1,0:T(8,128)(4,1)S(1)} %copy.52), kind=kOutput, calls=%fused_computation.2 | convolution fusion | flops 404226048 | bytes 6815792 | tf_op jit(solution)/shard_map/jsab,jsbm->jam/dot_general | solution.py:106
  135.3 2.9 copy.57
  138.2 8.9 %all-to-all-done.3 = f32[64,1,5120]{2,1,0:T(1,128)} async-done(((f32[64,1,5120]{2,1,0:T(1,128)}), f32[64,1,5120]{2,1,0:T(1,128)}, u32[]{:S(2)}, u32[]{:S(2)}) %all-to-all-start.3) | async-done | bytes 1310752 | tf_op jit(solution)/shard_map/all_to_all | solution.py:32
  147.2 1.6 copy.73
  148.7 0.3 broadcast_in_dim.51
  149.0 19.4 %all_to_all.57 = f32[2,64,5120]{2,1,0:T(8,128)S(1)} all-to-all(f32[2,64,5120]{2,1,0:T(8,128)S(1)} %broadcast_in_dim.51), channel_id=1, replica_groups=mesh['wire_0'=4,'wire_1'=4,'wire_2'=4,'wire_3'=2,'col'=2] {'wire_3'}, dimensions={0} | all-to-all | bytes 5242880 | tf_op jit(solution)/shard_map/all_to_all | solution.py:32
  168.4 3.6 %copy.56 = f32[64,2,5120]{2,1,0:T(2,128)} copy(f32[64,2,5120]{2,0,1:T(8,128)S(1)} %bitcast.54) | data formatting | bytes 5242880 | tf_op jit(solution)/shard_map/transpose | solution.py:51
  172.0 4.8 %slice.19 = f32[2560,256]{1,0:T(8,128)} reshape(f32[64,2,5120]{2,1,0:T(2,128)} %copy.56) | data formatting | bytes 5242880 | tf_op jit(solution)/shard_map/slice | solution.py:85
  176.7 7.0 %fusion.4 = f32[2048,256]{0,1:T(8,128)S(1)} fusion(f32[2048,256]{0,1:T(8,128)} %copy.57, bf16[2048,2048]{1,0:T(8,128)(2,1)} %param.7, f32[2560,256]{1,0:T(8,128)} %slice.19), kind=kOutput, calls=%fused_computation.9 | convolution fusion | flops 2148007936 | bytes 13631488 | tf_op jit(solution)/shard_map/dot_general | solution.py:116
  183.7 1.3 copy-done.2
  185.0 3.5 %convolution_bitcast_fusion.4 = f32[512,256]{0,1:T(8,128)S(1)} fusion(f32[2048,256]{0,1:T(8,128)S(1)} %fusion.4, bf16[2048,512]{0,1:T(8,128)(2,1)} %bitcast.7), kind=kOutput, calls=%fused_computation.16 | convolution fusion | flops 3221225472 | bytes 4718592 | tf_op jit(solution)/shard_map/dot_general | solution.py:118
  188.9 4.2 %all_to_all.58 = f32[2,64,4,256]{3,2,1,0:T(4,128)S(1)} all-to-all(f32[2,64,4,256]{3,2,1,0:T(4,128)S(1)} %copy.61), channel_id=1, replica_groups=mesh['wire_0'=4,'wire_1'=4,'wire_2'=4,'wire_3'=2,'col'=2] {'wire_3'}, dimensions={0} | all-to-all | bytes 1048576 | tf_op jit(solution)/shard_map/all_to_all | solution.py:63
  193.3 22.1 %all_to_all.59 = f32[64,4,256]{2,1,0:T(4,128)S(1)} all-to-all(f32[64,4,256]{2,1,0:T(4,128)S(1)} %reduce_sum.48), channel_id=1, replica_groups=mesh['wire_0'=4,'wire_1'=4,'wire_2'=4,'wire_3'=2,'col'=2] {'wire_0','wir..., dimensions={0} | all-to-all | bytes 524288 | tf_op jit(solution)/shard_map/all_to_all | solution.py:71
  215.5 0.8 broadcast_in_dim.52
  216.2 5.5 %all-to-all-start.8 = ((f32[64,4,256]{2,1,0:T(4,128)}), f32[64,4,256]{2,1,0:T(4,128)S(1)}, u32[]{:S(2)}, u32[]{:S(2)}) async-start(f32[64,4,256]{2,1,0:T(4,128)} %broadcast_in_dim.52), calls=%async_computation.8 | async-start | bytes 524288 | tf_op jit(solution)/shard_map/all_to_all | solution.py:32
  221.8 1.1 slice_multiply_fusion
  222.9 9.9 %convolution_bitcast_fusion = f32[2,2048,256]{2,1,0:T(8,128)} fusion(f32[2,256,256]{2,1,0:T(8,128)S(1)} %bitcast.61, f32[2048,256]{0,1:T(8,128)} %copy-done.2), kind=kOutput, calls=%fused_computation.1 | convolution fusion | flops 3221225472 | bytes 6815744 | tf_op jit(solution)/shard_map/dot_general | solution.py:122
  232.7 2.1 all-to-all-done.8
  234.9 6.1 %all_to_all.60 = f32[2,64,4,256]{3,2,1,0:T(4,128)S(1)} all-to-all(f32[2,64,4,256]{3,2,1,0:T(4,128)S(1)} %broadcast_in_dim.53), channel_id=1, replica_groups=mesh['wire_0'=4,'wire_1'=4,'wire_2'=4,'wire_3'=2,'col'=2] {'wire_3'}, dimensions={0} | all-to-all | bytes 1048576 | tf_op jit(solution)/shard_map/all_to_all | solution.py:32
  240.9 5.6 %all-to-all-start.5 = ((f32[2,2048,256]{2,1,0:T(8,128)}), f32[2,2048,256]{2,1,0:T(8,128)}, u32[]{:S(2)}, u32[]{:S(2)}) async-start(f32[2,2048,256]{2,1,0:T(8,128)} %convolution_bitcast_fusion), calls=%async_computation.5 | async-start | bytes 8388608 | tf_op jit(solution)/shard_map/all_to_all | solution.py:63
  246.9 46.8 %all-to-all-done.5 = f32[2,2048,256]{2,1,0:T(8,128)} async-done(((f32[2,2048,256]{2,1,0:T(8,128)}), f32[2,2048,256]{2,1,0:T(8,128)}, u32[]{:S(2)}, u32[]{:S(2)}) %all-to-all-start.5) | async-done | bytes 4194336 | tf_op jit(solution)/shard_map/all_to_all | solution.py:63
  293.7 4.1 %reduce_sum.47 = f32[2048,256]{1,0:T(8,128)} reduce(f32[2,2048,256]{2,1,0:T(8,128)} %all-to-all-done.5, f32[]{:T(128)} %constant.24.clone.1), dimensions={0}, to_apply=%region_2.3 | reduce | flops 524288 | bytes 6291460 | tf_op jit(solution)/shard_map/reduce_sum | solution.py:64
  297.7 2.9 copy.59
  300.6 6.2 %fusion.3 = f32[2048,256]{0,1:T(8,128)} fusion(f32[512,256]{1,0:T(8,128)S(1)} %div.13, bf16[2048,512]{0,1:T(8,128)(2,1)} %bitcast.7, f32[2048,256]{0,1:T(8,128)} %copy.59, f32[2048,256]{0,1:T(8,128)} %copy-done.2), kind=kOutput, calls=%fused_computation.7 | convolution fusion | flops 3222798336 | bytes 8912896 | tf_op jit(solution)/shard_map/dot_general | solution.py:125
  306.8 2.9 copy.64
  (28 shorter events, 1.4 us)
Async XLA Ops:
  0.0 131.3 %copy-start = (bf16[16,3,128,128]{3,2,1,0:T(8,128)(2,1)S(1)}, bf16[16,3,128,128]{3,2,1,0:T(8,128)(2,1)}, u32[]{:S(2)}) copy-start(bf16[16,3,128,128]{3,2,1,0:T(8,128)(2,1)} %param.5) | copy-start | bytes 4718596
  3.2 4.9 %copy-start.4 = (bf16[2048,256]{1,0:T(8,128)(2,1)S(1)}, bf16[2048,256]{1,0:T(8,128)(2,1)}, u32[]{:S(2)}) copy-start(bf16[2048,256]{1,0:T(8,128)(2,1)} %param.9) | copy-start | bytes 3145732
  3.2 28.8 %all-to-all-start = ((bf16[2,2048,256]{1,2,0:T(8,128)(2,1)}), bf16[2,2048,256]{1,2,0:T(8,128)(2,1)}, u32[]{:S(2)}, u32[]{:S(2)}) async-start(bf16[2,2048,256]{1,2,0:T(8,128)(2,1)} %broadcast_in_dim.48), calls=%async_computation | async-start | bytes 4194304 | tf_op jit(solution)/shard_map/all_to_all | solution.py:32
  32.0 2.7 copy-start.3
  109.6 11.3 %copy-start.5 = (s32[16,3]{0,1:T(4,128)S(1)}, s32[16,3]{0,1:T(4,128)}, u32[]{:S(2)}) copy-start(s32[16,3]{0,1:T(4,128)} %param.6) | copy-start | bytes 580
  111.4 35.8 %all-to-all-start.3 = ((f32[64,1,5120]{2,1,0:T(1,128)}), f32[64,1,5120]{2,1,0:T(1,128)}, u32[]{:S(2)}, u32[]{:S(2)}) async-start(f32[64,1,5120]{2,1,0:T(1,128)} %broadcast_in_dim.49), calls=%async_computation.3 | async-start | bytes 2621440 | tf_op jit(solution)/shard_map/all_to_all | solution.py:32
  118.5 6.5 %collective-permute-start = (bf16[256,256]{1,0:T(8,128)(2,1)S(1)}, bf16[256,256]{1,0:T(8,128)(2,1)S(1)}, u32[]{:S(2)}, u32[]{:S(2)}) collective-permute-start(bf16[256,256]{1,0:T(8,128)(2,1)S(1)} %get-tuple-element.5), channel_id=1, source_target_pairs={{0,2},{2,4},{4,6},{6,8},{8,10},{10,12},{12,14},{14,16},{16,18},{18... | collective-permute-start | bytes 393224 | tf_op jit(solution)/shard_map/ppermute | solution.py:18
  120.9 6.5 %collective-permute-start.1 = (bf16[256,256]{1,0:T(8,128)(2,1)S(1)}, bf16[256,256]{1,0:T(8,128)(2,1)S(1)}, u32[]{:S(2)}, u32[]{:S(2)}) collective-permute-start(bf16[256,256]{1,0:T(8,128)(2,1)S(1)} %get-tuple-element.6), channel_id=1, source_target_pairs={{2,0},{4,2},{6,4},{8,6},{10,8},{12,10},{14,12},{16,14},{18,16},{20... | collective-permute-start | bytes 393224 | tf_op jit(solution)/shard_map/ppermute | solution.py:19
  183.7 1.3 copy-start.2
  216.2 18.6 %all-to-all-start.8 = ((f32[64,4,256]{2,1,0:T(4,128)}), f32[64,4,256]{2,1,0:T(4,128)S(1)}, u32[]{:S(2)}, u32[]{:S(2)}) async-start(f32[64,4,256]{2,1,0:T(4,128)} %broadcast_in_dim.52), calls=%async_computation.8 | async-start | bytes 524288 | tf_op jit(solution)/shard_map/all_to_all | solution.py:32
  240.9 52.7 %all-to-all-start.5 = ((f32[2,2048,256]{2,1,0:T(8,128)}), f32[2,2048,256]{2,1,0:T(8,128)}, u32[]{:S(2)}, u32[]{:S(2)}) async-start(f32[2,2048,256]{2,1,0:T(8,128)} %convolution_bitcast_fusion), calls=%async_computation.5 | async-start | bytes 8388608 | tf_op jit(solution)/shard_map/all_to_all | solution.py:63
  300.6 9.1 %copy-start.1 = (bf16[16,3,128,128]{3,2,1,0:T(8,128)(2,1)S(1)}, bf16[16,3,128,128]{3,2,1,0:T(8,128)(2,1)}, u32[]{:S(2)}) copy-start(bf16[16,3,128,128]{3,2,1,0:T(8,128)(2,1)} %param.5) | copy-start | bytes 4718596
where the time goes:
time: 311 us; the launch traced here: 310 us
  blocking collectives  111 us (36%)
  waiting for transfers between devices  79.5 us (26%)
  local copies, waits for them, and re-layouts  41.2 us (13%)
  matrix products  38.8 us (12%)
  starting transfers between devices  25.5 us (8%)
  other arithmetic  13.7 us (4%)
    all_to_all x2, blocking collectives, summed_rows(): lax.all_to_all(nearer, far, split_axis=0, concat_axis=0, tiled=True)  71.5 us
    all_to_all x1, waiting for transfers between devices, summed_on_arrival(): lax.all_to_all(pieces, axis, split_axis=0, concat_axis=0, tiled=True)  46.8 us
    all_to_all x3, waiting for transfers between devices, sent_to_all(): lax.all_to_all(jnp.broadcast_to(shard[None], (devices, *shard.shape)), ax...  26.6 us
    all_to_all x2, blocking collectives, sent_to_all(): lax.all_to_all(jnp.broadcast_to(shard[None], (devices, *shard.shape)), ax...  25.5 us
    all_to_all x3, starting transfers between devices, sent_to_all(): lax.all_to_all(jnp.broadcast_to(shard[None], (devices, *shard.shape)), ax...  17.5 us
    all_to_all x2, blocking collectives, summed_on_arrival(): lax.all_to_all(pieces, axis, split_axis=0, concat_axis=0, tiled=True)  13.6 us
    dot_general x1, matrix products, body(): jnp.dot(image, intersection_scaled.T, precision=lax.Precision.HIGHEST)  9.88 us
    reduce_sum x3, other arithmetic, summed_on_arrival(): return arrived.sum(axis=0)  7.35 us
  transfers between devices with their start and end apart: 6, of which 6 were waited for; matrix products, arithmetic and copies ran while one was open for 10% of the time, Pallas kernels for 0%

commit v1 on v0

v1 whole, which is shorter than its diff:
```python
import jax
import jax.numpy as jnp
from jax import lax
from jax.experimental import pallas as pl
from jax.experimental.pallas import tpu as pltpu
from jax.sharding import Mesh
from jax.sharding import PartitionSpec as P

F32, BF16 = jnp.float32, jnp.bfloat16
MESH = pl.DeviceIdType.MESH
AXES = ("x", "zh", "y", "core", "zl")
WIRE = ("x", "zh", "y", "core")
SIDE, ZHI, ZALL = 4, 4, 8
LANES = 2
HALO, ROWS, COLS, KDIM, BLK = 256, 2048, 256, 2048, 128
HALF = KDIM // 2
TOTAL = 262144
TILE = 256


def mm(a, b):
    return jnp.dot(a, b, preferred_element_type=F32)


def mm_nt(a, b):
    return lax.dot_general(a, b, (((1,), (1,)), ((), ())), preferred_element_type=F32)


def split(v):
    hi = v.astype(BF16)
    return hi, (v - hi.astype(F32)).astype(BF16)


def at(start, size):
    return pl.ds(pl.multiple_of(start, size), size)


def near(src, i):
    return [src[at((i + r) * BLK, BLK), :] for r in range(5)]


def pick(blocks, shift):
    chosen = blocks[2]
    for r in (0, 1, 3, 4):
        chosen = jnp.where(shift == r - 2, blocks[r], chosen)
    return chosen


class Links:
    def __init__(self, send_sems, recv_sems):
        self.send_sems, self.recv_sems, self.started = send_sems, recv_sems, []

    def send(self, src, dst, **where):
        i = len(self.started)
        copy = pltpu.make_async_remote_copy(
            src_ref=src,
            dst_ref=dst,
            send_sem=self.send_sems.at[i],
            recv_sem=self.recv_sems.at[i],
            device_id=where,
            device_id_type=MESH,
        )
        copy.start()
        self.started.append(copy)
        return copy

    def finish(self):
        for copy in self.started:
            copy.wait_send()


N_SEMS = 160


def kernel(
    ham, off, phase_l, phase_r, orb, out,
    o_m, o_o, ot_m, ot_o, pr, plv, hv,
    core_tx, core_rx, acc, rx1, s1, rx2, s2, rx3, ct, band,
    s_q, s_crx, s_acc, s_rx1, s_s1, s_rx2, s_z, s_res,
    c_q, c_crx, c_acc, c_rx1, c_s1, c_rx2, c_z, c_res,
    d_hi, d_lo, y_hi, y_lo,
    load_sems, send_sems, recv_sems,
):
    at_axis = {a: lax.axis_index(a) for a in AXES}
    core, zl, zh = at_axis["core"], at_axis["zl"], at_axis["zh"]
    other = 1 - core
    z = zh * 2 + zl
    wire = ((at_axis["x"] * ZHI + zh) * SIDE + at_axis["y"]) * 2 + core
    n_wire = 128

    def step(axis, d):
        return {axis: lax.rem(at_axis[axis] + d, SIDE)}

    def along_z(d):
        there = lax.rem(z + d, ZALL)
        return {"zh": there // 2, "zl": lax.rem(there, 2)}

    def on_wire(d):
        w = lax.rem(wire + d + n_wire, n_wire)
        return {
            "x": w // (ZHI * SIDE * 2),
            "zh": lax.rem(w // (SIDE * 2), ZHI),
            "y": lax.rem(w // 2, SIDE),
            "core": lax.rem(w, 2),
        }

    links = Links(send_sems, recv_sems)
    own = pl.ds(HALO, ROWS)

    def load(src, dst, i):
        copy = pltpu.make_async_copy(src, dst, load_sems.at[i])
        copy.start()
        return copy

    get_o = load(orb, o_m.at[own, :], 0)
    get_pr = []
    for i in range(4):
        start = (other if i < 2 else core) * HALF + (i % 2) * 512
        cols = at(start, 512)
        get_pr.append(load(phase_r.at[:, cols], pr.at[:, cols], 1 + i))
    get_h = load(ham, hv, 5)
    get_pl = load(phase_l, plv, 6)

    barrier = pltpu.get_barrier_semaphore()
    greeted = [step(a, d) for a in ("x", "y") for d in (1, 2, 3)]
    greeted += [along_z(d) for d in range(1, ZALL)]
    greeted += [{"core": other}, on_wire(1), on_wire(-1)]
    for where in greeted:
        pl.semaphore_signal(barrier, inc=1, device_id=where, device_id_type=MESH)

    get_o.wait()

    def turn(src, dst):
        @pl.loop(0, ROWS // TILE)
        def _(t):
            dst[:, at(t * TILE, TILE)] = src[pl.ds(pl.multiple_of(HALO + t * TILE, TILE), TILE), :].T

    turn(o_m, ot_m)
    pl.semaphore_wait(barrier, len(greeted))

    swap = links.send(o_m.at[own, :], o_o.at[own, :], zl=1 - zl)
    last, first = pl.ds(ROWS, HALO), pl.ds(HALO, HALO)
    before, after = pl.ds(0, HALO), pl.ds(HALO + ROWS, HALO)
    halo = [
        links.send(o_m.at[last, :], o_m.at[before, :], **on_wire(1)),
        links.send(o_m.at[first, :], o_m.at[after, :], **on_wire(-1)),
    ]

    def coupling(dst, j, k_start):
        @pl.loop(0, 2)
        def _(t):
            dst[:, at(j * 512 + t * TILE, TILE)] = mm(ot_m[...], pr[:, at(k_start + j * 512 + t * TILE, TILE)])

    to_core = []
    for j in range(2):
        get_pr[j].wait()
        coupling(core_tx, j, other * HALF)
        part = pl.ds(j * 512, 512)
        to_core.append(links.send(core_tx.at[:, part], core_rx.at[:, part], core=other))
    for j in range(2):
        get_pr[2 + j].wait()
        coupling(acc, j, core * HALF)

    first_axis, second_axis = ("x", "y"), ("y", "x")

    got1 = []
    for lane in range(LANES):
        part = pl.ds(lane * 512, 512)
        to_core[lane].wait_recv()
        acc[:, part] += core_rx[:, part]
        axis = first_axis[lane]
        got1.append([
            links.send(
                acc.at[:, at(lane * 512 + lax.rem(at_axis[axis] + d, SIDE) * BLK, BLK)],
                rx1.at[lane, d - 1],
                **step(axis, d),
            )
            for d in (1, 2, 3)
        ])

    get_h.wait()
    for copy in halo:
        copy.wait_recv()

    @pl.loop(0, ROWS // BLK)
    def _(i):
        blocks = near(o_m, i)
        total = mm(hv[i, 0], blocks[2])
        for s in (1, 2):
            total = total + mm(hv[i, s], pick(blocks, off[i, s]))
        band[at(i * BLK, BLK), :] = total

    got2 = []
    for lane in range(LANES):
        axis = second_axis[lane]
        for copy in got1[lane]:
            copy.wait_recv()
        mine = acc[:, at(lane * 512 + at_axis[first_axis[lane]] * BLK, BLK)]
        s1[lane] = (mine + rx1[lane, 0]) + (rx1[lane, 1] + rx1[lane, 2])
        got2.append([
            links.send(
                s1.at[lane, at(lax.rem(at_axis[axis] + d, SIDE) * 64, 64), :],
                rx2.at[lane, d - 1],
                **step(axis, d),
            )
            for d in (1, 2, 3)
        ])
    got3 = []
    for lane in range(LANES):
        for copy in got2[lane]:
            copy.wait_recv()
        mine = s1[lane, at(at_axis[second_axis[lane]] * 64, 64), :]
        s2[lane] = (mine + rx2[lane, 0]) + (rx2[lane, 1] + rx2[lane, 2])
        got3.append([
            links.send(
                s2.at[lane, at(lax.rem(zh + d, ZHI) * 16, 16), :],
                rx3.at[lane, d - 1],
                **step("zh", d),
            )
            for d in (1, 2, 3)
        ])

    def k_cols(lane):
        return at(core * HALF + lane * 512 + at_axis[first_axis[lane]] * BLK, BLK)

    def c_rows(lane):
        return at(at_axis[second_axis[lane]] * 64, 64)

    got4 = []
    for lane in range(LANES):
        for copy in got3[lane]:
            copy.wait_recv()
        mine = s2[lane, at(zh * 16, 16), :]
        piece = (mine + rx3[lane, 0]) + (rx3[lane, 1] + rx3[lane, 2])
        rows = at(at_axis[second_axis[lane]] * 64 + zh * 16, 16)
        ct[0, rows, k_cols(lane)] = piece.astype(BF16)
        got4.append([
            links.send(ct.at[0, rows, k_cols(lane)], ct.at[d % 2, rows, k_cols(lane)], **along_z(d))
            for d in range(1, ZALL)
        ])
    got5 = []
    for lane in range(LANES):
        for copy in got4[lane]:
            copy.wait_recv()
        block = ct.at[:, c_rows(lane), k_cols(lane)]
        got5.append([links.send(block, block, **step(second_axis[lane], d)) for d in (1, 2, 3)])
    got6 = []
    for lane in range(LANES):
        for copy in got5[lane]:
            copy.wait_recv()
        block = ct.at[:, :, k_cols(lane)]
        got6.append([links.send(block, block, **step(first_axis[lane], d)) for d in (1, 2, 3)])

    def summed(q, crx, part_acc, rx_a, sum_a, rx_b, z_b, res):
        mine_cols, other_cols = at(core * BLK, BLK), at(other * BLK, BLK)
        copy = links.send(q.at[:, other_cols], crx, core=other)
        yield
        copy.wait_recv()
        part_acc[...] = q[:, mine_cols] + crx[...]
        got = []
        for lane in range(LANES):
            axis = first_axis[lane]
            got.append([
                links.send(
                    part_acc.at[at(lane * 256 + lax.rem(at_axis[axis] + d, SIDE) * 64, 64), :],
                    rx_a.at[lane, d - 1],
                    **step(axis, d),
                )
                for d in (1, 2, 3)
            ])
        yield
        got_b = []
        for lane in range(LANES):
            for copy in got[lane]:
                copy.wait_recv()
            mine = part_acc[at(lane * 256 + at_axis[first_axis[lane]] * 64, 64), :]
            sum_a[lane] = (mine + rx_a[lane, 0]) + (rx_a[lane, 1] + rx_a[lane, 2])
            axis = second_axis[lane]
            got_b.append([
                links.send(
                    sum_a.at[lane, at(lax.rem(at_axis[axis] + d, SIDE) * 16, 16), :],
                    rx_b.at[lane, d - 1],
                    **step(axis, d),
                )
                for d in (1, 2, 3)
            ])
        yield
        got_z = []
        for lane in range(LANES):
            for copy in got_b[lane]:
                copy.wait_recv()
            mine = sum_a[lane, at(at_axis[second_axis[lane]] * 16, 16), :]
            z_b[lane, zh] = (mine + rx_b[lane, 0]) + (rx_b[lane, 1] + rx_b[lane, 2])
            got_z.append([links.send(z_b.at[lane, zh], z_b.at[lane, zh], **step("zh", d)) for d in (1, 2, 3)])
        yield
        got_g = []
        for lane in range(LANES):
            for copy in got_z[lane]:
                copy.wait_recv()
            rows = at(lane * 256 + at_axis[first_axis[lane]] * 64 + at_axis[second_axis[lane]] * 16, 16)
            res[rows, mine_cols] = (z_b[lane, 0] + z_b[lane, 1]) + (z_b[lane, 2] + z_b[lane, 3])
            block = res.at[rows, mine_cols]
            got_g.append([links.send(block, block, **step(second_axis[lane], d)) for d in (1, 2, 3)])
        yield
        got_h = []
        for lane in range(LANES):
            for copy in got_g[lane]:
                copy.wait_recv()
            block = res.at[at(lane * 256 + at_axis[first_axis[lane]] * 64, 64), mine_cols]
            got_h.append([links.send(block, block, **step(first_axis[lane], d)) for d in (1, 2, 3)])
        yield
        for lane in range(LANES):
            for copy in got_h[lane]:
                copy.wait_recv()
        block = res.at[:, mine_cols]
        copy = links.send(block, block, core=other)
        yield
        copy.wait_recv()
        yield

    swap.wait_recv()
    halo_o = [
        links.send(o_o.at[last, :], o_o.at[before, :], **on_wire(1)),
        links.send(o_o.at[first, :], o_o.at[after, :], **on_wire(-1)),
    ]
    turn(o_o, ot_o)
    s_q[:COLS, :] = mm(ot_m[...], o_m[own, :])
    s_q[COLS:, :] = mm(ot_o[...], o_m[own, :])
    s_sum = summed(s_q, s_crx, s_acc, s_rx1, s_s1, s_rx2, s_z, s_res)
    next(s_sum)

    got7 = []
    for lane in range(LANES):
        for copy in got6[lane]:
            copy.wait_recv()
        block = ct.at[:, :, at(core * HALF + lane * 512, 512)]
        got7.append(links.send(block, block, core=other))
    next(s_sum)
    for copy in got7:
        copy.wait_recv()
    get_pl.wait()

    c_q[...] = jnp.zeros_like(c_q)

    @pl.loop(0, ROWS // TILE)
    def _(t):
        rows = at(t * TILE, TILE)
        image = band[rows, :] + mm_nt(plv[rows, :], ct[0])
        hi, lo = split(image)
        c_q[:COLS, :] += mm(ot_m[:, rows], hi) + mm(ot_m[:, rows], lo)
        c_q[COLS:, :] += mm(ot_o[:, rows], hi) + mm(ot_o[:, rows], lo)

    c_sum = summed(c_q, c_crx, c_acc, c_rx1, c_s1, c_rx2, c_z, c_res)
    next(c_sum)
    for _ in range(6):
        next(s_sum)
        next(c_sum)

    for copy in halo_o:
        copy.wait_recv()
    scale = 1.0 / TOTAL
    row = lax.broadcasted_iota(jnp.int32, (COLS, COLS), 0)
    col = lax.broadcasted_iota(jnp.int32, (COLS, COLS), 1)
    m_m = jnp.where(row == col, 2.0, 0.0) - s_res[:COLS, :] * scale
    m_o = 0.0 - s_res[COLS:, :] * scale
    mm_hi, mm_lo = split(m_m)
    mo_hi, mo_lo = split(m_o)
    tm_hi, tm_lo = split(m_m.T)
    to_hi, to_lo = split(m_o.T)

    @pl.loop(0, (ROWS + 2 * HALO) // TILE)
    def _(t):
        rows = at(t * TILE, TILE)
        a, b = o_m[rows, :], o_o[rows, :]
        y = (mm(a, mm_hi) + mm(b, mo_hi)) + (mm(a, mm_lo) + mm(b, mo_lo))
        y_hi[rows, :], y_lo[rows, :] = split(y)

    @pl.loop(0, KDIM // TILE)
    def _(t):
        cols = at(t * TILE, TILE)
        a, b = ct[0, :, cols], ct[1, :, cols]
        d = (mm(tm_hi, a) + mm(to_hi, b)) + (mm(tm_lo, a) + mm(to_lo, b))
        d_hi[:, cols], d_lo[:, cols] = split(d)

    @pl.loop(0, ROWS // BLK)
    def _(i):
        total = None
        for src in (y_lo, y_hi):
            blocks = near(src, i)
            term = mm(hv[i, 0], blocks[2])
            for s in (1, 2):
                term = term + mm(hv[i, s], pick(blocks, off[i, s]))
            total = term if total is None else total + term
        out[at(i * BLK, BLK), :] = total

    @pl.loop(0, ROWS // TILE)
    def _(t):
        rows = at(t * TILE, TILE)
        out[rows, :] += mm_nt(plv[rows, :], d_hi[...]) + mm_nt(plv[rows, :], d_lo[...])

    next(c_sum)
    xm_hi, xm_lo = split(c_res[:COLS, :] * scale)
    xo_hi, xo_lo = split(c_res[COLS:, :] * scale)

    @pl.loop(0, ROWS // TILE)
    def _(t):
        rows = at(t * TILE, TILE)
        inner = pl.ds(pl.multiple_of(HALO + t * TILE, TILE), TILE)
        a, b = o_m[inner, :], o_o[inner, :]
        out[rows, :] -= (mm(a, xm_hi) + mm(b, xo_hi)) + (mm(a, xm_lo) + mm(b, xo_lo))

    links.finish()


def body(hamiltonian, offsets, phase_left, phase_right, orbitals):
    def sums():
        return [
            pltpu.VMEM((512, 256), F32),
            pltpu.VMEM((512, 128), F32),
            pltpu.VMEM((512, 128), F32),
            pltpu.VMEM((2, 3, 64, 128), F32),
            pltpu.VMEM((2, 64, 128), F32),
            pltpu.VMEM((2, 3, 16, 128), F32),
            pltpu.VMEM((2, 4, 16, 128), F32),
            pltpu.VMEM((512, 256), F32),
        ]

    hbm = pl.BlockSpec(memory_space=pl.ANY)
    return pl.pallas_call(
        kernel,
        out_shape=jax.ShapeDtypeStruct((ROWS, COLS), F32),
        in_specs=[hbm, pl.BlockSpec(memory_space=pltpu.SMEM), hbm, hbm, hbm],
        out_specs=pl.BlockSpec(memory_space=pltpu.VMEM),
        scratch_shapes=[
            pltpu.VMEM((ROWS + 2 * HALO, COLS), BF16),
            pltpu.VMEM((ROWS + 2 * HALO, COLS), BF16),
            pltpu.VMEM((COLS, ROWS), BF16),
            pltpu.VMEM((COLS, ROWS), BF16),
            pltpu.VMEM((ROWS, KDIM), BF16),
            pltpu.VMEM((ROWS, KDIM), BF16),
            pltpu.VMEM((16, 3, BLK, BLK), BF16),
            pltpu.VMEM((COLS, HALF), F32),
            pltpu.VMEM((COLS, HALF), F32),
            pltpu.VMEM((COLS, HALF), F32),
            pltpu.VMEM((2, 3, 256, 128), F32),
            pltpu.VMEM((2, 256, 128), F32),
            pltpu.VMEM((2, 3, 64, 128), F32),
            pltpu.VMEM((2, 64, 128), F32),
            pltpu.VMEM((2, 3, 16, 128), F32),
            pltpu.VMEM((2, COLS, KDIM), BF16),
            pltpu.VMEM((ROWS, COLS), F32),
            *sums(),
            *sums(),
            pltpu.VMEM((COLS, KDIM), BF16),
            pltpu.VMEM((COLS, KDIM), BF16),
            pltpu.VMEM((ROWS + 2 * HALO, COLS), BF16),
            pltpu.VMEM((ROWS + 2 * HALO, COLS), BF16),
            pltpu.SemaphoreType.DMA((8,)),
            pltpu.SemaphoreType.DMA((N_SEMS,)),
            pltpu.SemaphoreType.DMA((N_SEMS,)),
        ],
        compiler_params=pltpu.CompilerParams(
            collective_id=0, has_side_effects=True, vmem_limit_bytes=58 << 20
        ),
        cost_estimate=pl.CostEstimate(flops=16 * 10**9, bytes_accessed=20 * 2**20, transcendentals=0),
    )(hamiltonian, offsets, phase_left, phase_right, orbitals)


def solution(mesh):
    finer = Mesh(mesh.devices.reshape(SIDE, ZHI, SIDE, 2, mesh.shape["col"]), AXES)
    in_specs = (
        P(WIRE, None, None, None),
        P(WIRE, None),
        P(WIRE, None),
        P(WIRE, None),
        P(WIRE, "zl"),
    )
    return jax.shard_map(body, mesh=finer, in_specs=in_specs, out_specs=P(WIRE, "zl"), check_vma=False)
```

time: 311 us -> 127 us (0.41)
  Pallas kernels: 0 us -> 121 us
  blocking collectives: 111 us -> 0 us
  waiting for transfers between devices: 79.5 us -> 0 us
  matrix products: 38.8 us -> 0 us
  local copies, waits for them, and re-layouts: 41.2 us -> 4.4 us
  starting transfers between devices: 25.5 us -> 0 us
  other arithmetic: 13.7 us -> 0 us
    pallas_call x0 -> x1, Pallas kernels: none -> 121 us  [body(): pl.pallas_call(kernel, out_shape=jax.ShapeDtypeStruct((ROWS, COLS), F32),...]
    all_to_all x6 -> x0, blocking collectives: 111 us -> none  [the longest x2 71.5 us: summed_rows(): lax.all_to_all(nearer, far, split_axis=0, concat_axis=0, tiled=True)]
    all_to_all x4 -> x0, waiting for transfers between devices: 73.3 us -> none  [the longest x1 46.8 us: summed_on_arrival(): lax.all_to_all(pieces, axis, split_axis=0, concat_axis=0, tiled=True)]
    dot_general x7 -> x0, matrix products: 38.8 us -> none  [the longest x1 9.88 us: body(): jnp.dot(image, intersection_scaled.T, precision=lax.Precision.HIGHEST)]
    all_to_all x4 -> x0, starting transfers between devices: 23.1 us -> none  [the longest x3 17.5 us: sent_to_all(): lax.all_to_all(jnp.broadcast_to(shard[None], (devices, *shard.shape)), ax...]
    reduce_sum x5 -> x0, other arithmetic: 9.51 us -> none  [the longest x3 7.35 us: summed_on_arrival(): return arrived.sum(axis=0)]
    ppermute x2 -> x0, waiting for transfers between devices: 6.19 us -> none  [the longest x1 3.77 us: padded_2(): before = lax.ppermute(last, axis, up)]
    transpose x3 -> x0, local copies, waits for them, and re-layouts: 6.19 us -> none  [the longest x1 3.57 us: gathered_by_axis(): pieces = jnp.swapaxes(sent_to_all(leading, near), 0, 1)]
  transfers between devices with their start and end apart: 6 -> 0, of which waited for: 6 -> 0; matrix products, arithmetic and copies ran while one was open for 10% -> 0% of each run, Pallas kernels for 0% -> 0%
where the time goes in v1:
time: 127 us; the launch traced here: 125 us
  Pallas kernels  121 us (95%)
  local copies, waits for them, and re-layouts  4.4 us (3%)
    pallas_call x1, Pallas kernels, body(): pl.pallas_call(kernel, out_shape=jax.ShapeDtypeStruct((ROWS, COLS), F32),...  121 us
    unnamed x2, local copies, waits for them, and re-layouts  4.4 us

profile of v1, /device:TPU:1, one launch (start us, length us, event | category | flops | bytes accessed | tf_op | source)
XLA Modules:
  0.0 125.1 jit_solution(14663351159872192426)
XLA Ops:
  0.0 1.4 %copy.6.off = s32[16,3]{1,0:T(8,128)} copy(s32[16,3]{0,1:T(4,128)} %param.6) | data formatting | bytes 384 | tf_op args[1]
  1.4 120.6 %shard_map.55 = f32[2048,256]{1,0:T(8,128)} custom-call(bf16[16,3,128,128]{3,2,1,0:T(8,128)(2,1)} %ham.1, s32[16,3]{1,0:T(8,128)} %copy.6.off, bf16[2048,2048]{1,0:T(8,128)(2,1)} %phase_l.1, bf16[2048,2048]{1,0:T(8,128)(2,1)} %phase_r.1, bf16[2048,256]{1,0:T(8,128)(2,1)} %orb.1), custom_call_target="tpu_custom_call" | custom-call | flops 16000000000 | bytes 20971520 | tf_op jit(solution)/shard_map/pallas_call | solution.py:429
  122.0 3.0 %copy.8 = f32[2048,256]{1,0:T(8,128)} copy(f32[2048,256]{1,0:T(8,128)} %shard_map.55) | data formatting | bytes 4194304

commit v2 on v1

--- a/solution.py
+++ b/solution.py
@@ -73,12 +73,12 @@
 
 
 def kernel(
-    ham, off, phase_l, phase_r, orb, out,
-    o_m, o_o, ot_m, ot_o, pr, plv, hv,
-    core_tx, core_rx, acc, rx1, s1, rx2, s2, rx3, ct, band,
+    ham, off, phase_l, phase_r, orb, base, cols_o, cross,
+    o_m, o_o, ot, pr, plv, hv,
+    core_tx, core_rx, acc, rx1, s1, rx2, s2, rx3, ct, image, im_hi, im_lo,
     s_q, s_crx, s_acc, s_rx1, s_s1, s_rx2, s_z, s_res,
     c_q, c_crx, c_acc, c_rx1, c_s1, c_rx2, c_z, c_res,
-    d_hi, d_lo, y_hi, y_lo,
+    d2, y_hi, y_lo, rest,
     load_sems, send_sems, recv_sems,
 ):
     at_axis = {a: lax.axis_index(a) for a in AXES}
@@ -86,7 +86,7 @@
     other = 1 - core
     z = zh * 2 + zl
     wire = ((at_axis["x"] * ZHI + zh) * SIDE + at_axis["y"]) * 2 + core
-    n_wire = 128
+    n_wire = SIDE * ZHI * SIDE * 2
 
     def step(axis, d):
         return {axis: lax.rem(at_axis[axis] + d, SIDE)}
@@ -118,51 +118,51 @@
         start = (other if i < 2 else core) * HALF + (i % 2) * 512
         cols = at(start, 512)
         get_pr.append(load(phase_r.at[:, cols], pr.at[:, cols], 1 + i))
-    get_h = load(ham, hv, 5)
-    get_pl = load(phase_l, plv, 6)
-
     barrier = pltpu.get_barrier_semaphore()
     greeted = [step(a, d) for a in ("x", "y") for d in (1, 2, 3)]
     greeted += [along_z(d) for d in range(1, ZALL)]
     greeted += [{"core": other}, on_wire(1), on_wire(-1)]
     for where in greeted:
         pl.semaphore_signal(barrier, inc=1, device_id=where, device_id_type=MESH)
-
     get_o.wait()
 
-    def turn(src, dst):
-        @pl.loop(0, ROWS // TILE)
+    def turn(src, top):
+        @pl.loop(0, ROWS // 512)
         def _(t):
-            dst[:, at(t * TILE, TILE)] = src[pl.ds(pl.multiple_of(HALO + t * TILE, TILE), TILE), :].T
-
-    turn(o_m, ot_m)
+            inner = pl.ds(pl.multiple_of(HALO + t * 512, TILE), 512)
+            ot[top : top + COLS, at(t * 512, 512)] = src[inner, :].T
+
+    turn(o_m, 0)
+
+    def coupling(dst, j, k_start):
+        dst[:, j * 512 : (j + 1) * 512] = mm(ot[:COLS, :], pr[:, at(k_start + j * 512, 512)])
+
+    get_pr[0].wait()
+    coupling(core_tx, 0, other * HALF)
     pl.semaphore_wait(barrier, len(greeted))
 
-    swap = links.send(o_m.at[own, :], o_o.at[own, :], zl=1 - zl)
+    def core_send(j):
+        part = pl.ds(j * 512, 512)
+        return links.send(core_tx.at[:, part], core_rx.at[:, part], core=other)
+
     last, first = pl.ds(ROWS, HALO), pl.ds(HALO, HALO)
     before, after = pl.ds(0, HALO), pl.ds(HALO + ROWS, HALO)
+    to_core = [core_send(0)]
     halo = [
         links.send(o_m.at[last, :], o_m.at[before, :], **on_wire(1)),
         links.send(o_m.at[first, :], o_m.at[after, :], **on_wire(-1)),
     ]
-
-    def coupling(dst, j, k_start):
-        @pl.loop(0, 2)
-        def _(t):
-            dst[:, at(j * 512 + t * TILE, TILE)] = mm(ot_m[...], pr[:, at(k_start + j * 512 + t * TILE, TILE)])
-
-    to_core = []
-    for j in range(2):
-        get_pr[j].wait()
-        coupling(core_tx, j, other * HALF)
-        part = pl.ds(j * 512, 512)
-        to_core.append(links.send(core_tx.at[:, part], core_rx.at[:, part], core=other))
+    swap = links.send(o_m.at[own, :], o_o.at[own, :], zl=1 - zl)
+    get_pr[1].wait()
+    coupling(core_tx, 1, other * HALF)
+    to_core.append(core_send(1))
     for j in range(2):
         get_pr[2 + j].wait()
         coupling(acc, j, core * HALF)
+    get_h = load(ham, hv, 5)
+    get_pl = load(phase_l, plv, 6)
 
     first_axis, second_axis = ("x", "y"), ("y", "x")
-
     got1 = []
     for lane in range(LANES):
         part = pl.ds(lane * 512, 512)
@@ -177,19 +177,6 @@
             )
             for d in (1, 2, 3)
         ])
-
-    get_h.wait()
-    for copy in halo:
-        copy.wait_recv()
-
-    @pl.loop(0, ROWS // BLK)
-    def _(i):
-        blocks = near(o_m, i)
-        total = mm(hv[i, 0], blocks[2])
-        for s in (1, 2):
-            total = total + mm(hv[i, s], pick(blocks, off[i, s]))
-        band[at(i * BLK, BLK), :] = total
-
     got2 = []
     for lane in range(LANES):
         axis = second_axis[lane]
@@ -244,12 +231,6 @@
             copy.wait_recv()
         block = ct.at[:, c_rows(lane), k_cols(lane)]
         got5.append([links.send(block, block, **step(second_axis[lane], d)) for d in (1, 2, 3)])
-    got6 = []
-    for lane in range(LANES):
-        for copy in got5[lane]:
-            copy.wait_recv()
-        block = ct.at[:, :, k_cols(lane)]
-        got6.append([links.send(block, block, **step(first_axis[lane], d)) for d in (1, 2, 3)])
 
     def summed(q, crx, part_acc, rx_a, sum_a, rx_b, z_b, res):
         mine_cols, other_cols = at(core * BLK, BLK), at(other * BLK, BLK)
@@ -318,17 +299,37 @@
         copy.wait_recv()
         yield
 
+    got6 = []
+    for lane in range(LANES):
+        for copy in got5[lane]:
+            copy.wait_recv()
+        block = ct.at[:, :, k_cols(lane)]
+        got6.append([links.send(block, block, **step(first_axis[lane], d)) for d in (1, 2, 3)])
+
     swap.wait_recv()
+    put_o = load(o_o.at[own, :], cols_o, 7)
     halo_o = [
         links.send(o_o.at[last, :], o_o.at[before, :], **on_wire(1)),
         links.send(o_o.at[first, :], o_o.at[after, :], **on_wire(-1)),
     ]
-    turn(o_o, ot_o)
-    s_q[:COLS, :] = mm(ot_m[...], o_m[own, :])
-    s_q[COLS:, :] = mm(ot_o[...], o_m[own, :])
+    turn(o_o, COLS)
+    s_q[...] = mm(ot[...], o_m[own, :])
     s_sum = summed(s_q, s_crx, s_acc, s_rx1, s_s1, s_rx2, s_z, s_res)
     next(s_sum)
 
+    get_h.wait()
+    for copy in halo:
+        copy.wait_recv()
+
+    @pl.loop(0, ROWS // BLK)
+    def _(i):
+        blocks = near(o_m, i)
+        total = mm(hv[i, 0], blocks[2])
+        for s in (1, 2):
+            total = total + mm(hv[i, s], pick(blocks, off[s, i]))
+        image[at(i * BLK, BLK), :] = total
+
+    next(s_sum)
     got7 = []
     for lane in range(LANES):
         for copy in got6[lane]:
@@ -336,28 +337,35 @@
         block = ct.at[:, :, at(core * HALF + lane * 512, 512)]
         got7.append(links.send(block, block, core=other))
     next(s_sum)
+    get_pl.wait()
+
+    k_mine, k_other = at(core * HALF, HALF), at(other * HALF, HALF)
+
+    @pl.loop(0, ROWS // 1024)
+    def _(t):
+        rows = at(t * 1024, 1024)
+        image[rows, :] += mm_nt(plv[rows, k_mine], ct[0, :, k_mine])
+
     for copy in got7:
         copy.wait_recv()
-    get_pl.wait()
-
-    c_q[...] = jnp.zeros_like(c_q)
-
-    @pl.loop(0, ROWS // TILE)
+
+    @pl.loop(0, ROWS // 1024)
     def _(t):
-        rows = at(t * TILE, TILE)
-        image = band[rows, :] + mm_nt(plv[rows, :], ct[0])
-        hi, lo = split(image)
-        c_q[:COLS, :] += mm(ot_m[:, rows], hi) + mm(ot_m[:, rows], lo)
-        c_q[COLS:, :] += mm(ot_o[:, rows], hi) + mm(ot_o[:, rows], lo)
-
+        rows = at(t * 1024, 1024)
+        im_hi[rows, :], im_lo[rows, :] = split(image[rows, :] + mm_nt(plv[rows, k_other], ct[0, :, k_other]))
+
+    c_q[...] = mm(ot[...], im_hi[...]) + mm(ot[...], im_lo[...])
     c_sum = summed(c_q, c_crx, c_acc, c_rx1, c_s1, c_rx2, c_z, c_res)
     next(c_sum)
-    for _ in range(6):
-        next(s_sum)
-        next(c_sum)
-
-    for copy in halo_o:
-        copy.wait_recv()
+    next(s_sum)
+    next(c_sum)
+    next(s_sum)
+    next(c_sum)
+    next(s_sum)
+    next(c_sum)
+    next(s_sum)
+    next(s_sum)
+
     scale = 1.0 / TOTAL
     row = lax.broadcasted_iota(jnp.int32, (COLS, COLS), 0)
     col = lax.broadcasted_iota(jnp.int32, (COLS, COLS), 1)
@@ -368,19 +376,25 @@
     tm_hi, tm_lo = split(m_m.T)
     to_hi, to_lo = split(m_o.T)
 
-    @pl.loop(0, (ROWS + 2 * HALO) // TILE)
+    @pl.loop(0, KDIM // 512)
     def _(t):
-        rows = at(t * TILE, TILE)
+        cols = at(t * 512, 512)
+        a, b = ct[0, :, cols], ct[1, :, cols]
+        d = (mm(tm_hi, a) + mm(to_hi, b)) + (mm(tm_lo, a) + mm(to_lo, b))
+        d2[:COLS, cols], d2[COLS:, cols] = split(d)
+
+    next(c_sum)
+    for copy in halo_o:
+        copy.wait_recv()
+
+    @pl.loop(0, (ROWS + 2 * HALO) // 512)
+    def _(t):
+        rows = at(t * 512, 512)
         a, b = o_m[rows, :], o_o[rows, :]
         y = (mm(a, mm_hi) + mm(b, mo_hi)) + (mm(a, mm_lo) + mm(b, mo_lo))
         y_hi[rows, :], y_lo[rows, :] = split(y)
 
-    @pl.loop(0, KDIM // TILE)
-    def _(t):
-        cols = at(t * TILE, TILE)
-        a, b = ct[0, :, cols], ct[1, :, cols]
-        d = (mm(tm_hi, a) + mm(to_hi, b)) + (mm(tm_lo, a) + mm(to_lo, b))
-        d_hi[:, cols], d_lo[:, cols] = split(d)
+    next(c_sum)
 
     @pl.loop(0, ROWS // BLK)
     def _(i):
@@ -389,27 +403,34 @@
             blocks = near(src, i)
             term = mm(hv[i, 0], blocks[2])
             for s in (1, 2):
-                term = term + mm(hv[i, s], pick(blocks, off[i, s]))
+                term = term + mm(hv[i, s], pick(blocks, off[s, i]))
             total = term if total is None else total + term
-        out[at(i * BLK, BLK), :] = total
-
-    @pl.loop(0, ROWS // TILE)
+        rest[at(i * BLK, BLK), :] = total
+
+    next(c_sum)
+
+    @pl.loop(0, ROWS // 512)
     def _(t):
-        rows = at(t * TILE, TILE)
-        out[rows, :] += mm_nt(plv[rows, :], d_hi[...]) + mm_nt(plv[rows, :], d_lo[...])
-
-    next(c_sum)
-    xm_hi, xm_lo = split(c_res[:COLS, :] * scale)
-    xo_hi, xo_lo = split(c_res[COLS:, :] * scale)
-
-    @pl.loop(0, ROWS // TILE)
-    def _(t):
-        rows = at(t * TILE, TILE)
-        inner = pl.ds(pl.multiple_of(HALO + t * TILE, TILE), TILE)
-        a, b = o_m[inner, :], o_o[inner, :]
-        out[rows, :] -= (mm(a, xm_hi) + mm(b, xo_hi)) + (mm(a, xm_lo) + mm(b, xo_lo))
-
+        rows = at(t * 512, 512)
+        both = mm_nt(plv[rows, :], d2[...])
+        rest[rows, :] += both[:, :COLS] + both[:, COLS:]
+
+    put_base = load(rest, base, 8)
+    next(c_sum)
+    put_cross = load(c_res, cross, 9)
+    for copy in (put_o, put_base, put_cross):
+        copy.wait()
     links.finish()
+
+
+def last_kernel(base, o_m, o_o, cross, out, x_hi, x_lo):
+    @pl.when(pl.program_id(0) == 0)
+    def _():
+        x_hi[...], x_lo[...] = split(cross[...] * (1.0 / TOTAL))
+
+    a, b = o_m[...], o_o[...]
+    low = mm(a, x_lo[:COLS, :]) + mm(b, x_lo[COLS:, :])
+    out[...] = base[...] - ((mm(a, x_hi[:COLS, :]) + mm(b, x_hi[COLS:, :])) + low)
 
 
 def body(hamiltonian, offsets, phase_left, phase_right, orbitals):
@@ -426,16 +447,19 @@
         ]
 
     hbm = pl.BlockSpec(memory_space=pl.ANY)
-    return pl.pallas_call(
+    base, cols_o, cross = pl.pallas_call(
         kernel,
-        out_shape=jax.ShapeDtypeStruct((ROWS, COLS), F32),
+        out_shape=[
+            jax.ShapeDtypeStruct((ROWS, COLS), F32),
+            jax.ShapeDtypeStruct((ROWS, COLS), BF16),
+            jax.ShapeDtypeStruct((2 * COLS, COLS), F32),
+        ],
         in_specs=[hbm, pl.BlockSpec(memory_space=pltpu.SMEM), hbm, hbm, hbm],
-        out_specs=pl.BlockSpec(memory_space=pltpu.VMEM),
+        out_specs=[hbm, hbm, hbm],
         scratch_shapes=[
             pltpu.VMEM((ROWS + 2 * HALO, COLS), BF16),
             pltpu.VMEM((ROWS + 2 * HALO, COLS), BF16),
-            pltpu.VMEM((COLS, ROWS), BF16),
-            pltpu.VMEM((COLS, ROWS), BF16),
+            pltpu.VMEM((2 * COLS, ROWS), BF16),
             pltpu.VMEM((ROWS, KDIM), BF16),
             pltpu.VMEM((ROWS, KDIM), BF16),
             pltpu.VMEM((16, 3, BLK, BLK), BF16),
@@ -449,13 +473,15 @@
             pltpu.VMEM((2, 3, 16, 128), F32),
             pltpu.VMEM((2, COLS, KDIM), BF16),
             pltpu.VMEM((ROWS, COLS), F32),
+            pltpu.VMEM((ROWS, COLS), BF16),
+            pltpu.VMEM((ROWS, COLS), BF16),
             *sums(),
             *sums(),
-            pltpu.VMEM((COLS, KDIM), BF16),
-            pltpu.VMEM((COLS, KDIM), BF16),
+            pltpu.VMEM((2 * COLS, KDIM), BF16),
             pltpu.VMEM((ROWS + 2 * HALO, COLS), BF16),
             pltpu.VMEM((ROWS + 2 * HALO, COLS), BF16),
-            pltpu.SemaphoreType.DMA((8,)),
+            pltpu.VMEM((ROWS, COLS), F32),
+            pltpu.SemaphoreType.DMA((10,)),
             pltpu.SemaphoreType.DMA((N_SEMS,)),
             pltpu.SemaphoreType.DMA((N_SEMS,)),
         ],
@@ -463,7 +489,18 @@
             collective_id=0, has_side_effects=True, vmem_limit_bytes=58 << 20
         ),
         cost_estimate=pl.CostEstimate(flops=16 * 10**9, bytes_accessed=20 * 2**20, transcendentals=0),
-    )(hamiltonian, offsets, phase_left, phase_right, orbitals)
+    )(hamiltonian, offsets.T, phase_left, phase_right, orbitals)
+    tile = pl.BlockSpec((512, COLS), lambda i: (i, 0))
+    whole = pl.BlockSpec((2 * COLS, COLS), lambda i: (0, 0))
+    return pl.pallas_call(
+        last_kernel,
+        grid=(ROWS // 512,),
+        out_shape=jax.ShapeDtypeStruct((ROWS, COLS), F32),
+        in_specs=[tile, tile, tile, whole],
+        out_specs=tile,
+        scratch_shapes=[pltpu.VMEM((2 * COLS, COLS), BF16), pltpu.VMEM((2 * COLS, COLS), BF16)],
+        compiler_params=pltpu.CompilerParams(vmem_limit_bytes=24 << 20),
+    )(base, orbitals, cols_o, cross)
 
 
 def solution(mesh):

time: 127 us -> 103 us (0.81); the launches traced: 125 us -> 103 us
  Pallas kernels: 121 us -> 99.4 us
    pallas_call x1 -> x2, Pallas kernels: 121 us -> 99.4 us  [the longest x1 96.4 us: body(): pl.pallas_call(kernel, out_shape=[jax.ShapeDtypeStruct((ROWS, COLS), F32)...]
    unnamed x2 -> x8, local copies, waits for them, and re-layouts: 4.4 us -> 3.85 us
where the time goes in v2:
time: 103 us
  Pallas kernels  99.4 us (97%)
  local copies, waits for them, and re-layouts  3.85 us (4%)
    pallas_call x1, Pallas kernels, body(): pl.pallas_call(kernel, out_shape=[jax.ShapeDtypeStruct((ROWS, COLS), F32)...  96.4 us
    unnamed x8, local copies, waits for them, and re-layouts  3.85 us
    pallas_call x1, Pallas kernels, body(): pl.pallas_call(last_kernel, grid=(ROWS // 512,), out_shape=jax.ShapeDtype...  3.05 us

profile of v2, /device:TPU:1, one launch (start us, length us, event | category | flops | bytes accessed | tf_op | source)
XLA Modules:
  0.0 103.3 jit_solution(18277767574571530362)
XLA Ops:
  0.0 0.0 copy-start.1
  0.0 96.4 %shard_map.55 = (f32[2048,256]{1,0:T(8,128)}, bf16[2048,256]{1,0:T(8,128)(2,1)}, f32[512,256]{1,0:T(8,128)}) custom-call(bf16[16,3,128,128]{3,2,1,0:T(8,128)(2,1)} %ham.1, s32[3,16]{1,0:T(4,128)} %bitcast.1, bf16[2048,2048]{1,0:T(8,128)(2,1)} %phase_l.1, bf16[2048,2048]{1,0:T(8,128)(2,1)} %phase_r.1, bf16[2048,256]{1,0:T(8,128)(2,1)} %o_m.1), custom_call_target="tpu_custom_call" | custom-call | flops 16000000000 | bytes 20971520 | tf_op jit(solution)/shard_map/pallas_call | solution.py:450
  96.4 0.0 copy-done.1
  96.4 0.0 copy-start
  96.4 1.6 %copy-done = f32[2048,256]{1,0:T(8,128)S(1)} copy-done((f32[2048,256]{1,0:T(8,128)S(1)}, f32[2048,256]{1,0:T(8,128)}, u32[]{:S(2)}) %copy-start) | copy-done | bytes 2097176
  98.0 0.0 copy-start.2
  98.0 1.2 %copy-done.2 = bf16[2048,256]{1,0:T(8,128)(2,1)S(1)} copy-done((bf16[2048,256]{1,0:T(8,128)(2,1)S(1)}, bf16[2048,256]{1,0:T(8,128)(2,1)}, u32[]{:S(2)}) %copy-start.2) | copy-done | bytes 1048600
  99.2 0.0 copy-start.3
  99.2 1.0 %copy-done.3 = f32[512,256]{1,0:T(8,128)S(1)} copy-done((f32[512,256]{1,0:T(8,128)S(1)}, f32[512,256]{1,0:T(8,128)}, u32[]{:S(2)}) %copy-start.3) | copy-done | bytes 524312
  100.2 3.1 %shard_map.56 = f32[2048,256]{1,0:T(8,128)} custom-call(f32[2048,256]{1,0:T(8,128)S(1)} %copy-done, bf16[2048,256]{1,0:T(8,128)(2,1)S(1)} %copy-done.1, bf16[2048,256]{1,0:T(8,128)(2,1)S(1)} %copy-done.2, f32[512,256]{1,0:T(8,128)S(1)} %copy-done.3), custom_call_target="tpu_custom_call" | custom-call | tf_op jit(solution)/shard_map/pallas_call | solution.py:495
Async XLA Ops:
  0.0 96.4 %copy-start.1 = (bf16[2048,256]{1,0:T(8,128)(2,1)S(1)}, bf16[2048,256]{1,0:T(8,128)(2,1)}, u32[]{:S(2)}) copy-start(bf16[2048,256]{1,0:T(8,128)(2,1)} %o_m.1) | copy-start | bytes 3145732
  96.4 1.6 %copy-start = (f32[2048,256]{1,0:T(8,128)S(1)}, f32[2048,256]{1,0:T(8,128)}, u32[]{:S(2)}) copy-start(f32[2048,256]{1,0:T(8,128)} %get-tuple-element.8.base) | copy-start | bytes 6291460
  98.0 1.2 %copy-start.2 = (bf16[2048,256]{1,0:T(8,128)(2,1)S(1)}, bf16[2048,256]{1,0:T(8,128)(2,1)}, u32[]{:S(2)}) copy-start(bf16[2048,256]{1,0:T(8,128)(2,1)} %get-tuple-element.9.o_o) | copy-start | bytes 3145732
  99.2 1.0 %copy-start.3 = (f32[512,256]{1,0:T(8,128)S(1)}, f32[512,256]{1,0:T(8,128)}, u32[]{:S(2)}) copy-start(f32[512,256]{1,0:T(8,128)} %get-tuple-element.10.cross) | copy-start | bytes 1572868

commit v3 on v2

--- a/solution.py
+++ b/solution.py
@@ -70,6 +70,7 @@
 
 
 N_SEMS = 160
+EARLY, LATE = 256, 768
 
 
 def kernel(
@@ -78,7 +79,7 @@
     core_tx, core_rx, acc, rx1, s1, rx2, s2, rx3, ct, image, im_hi, im_lo,
     s_q, s_crx, s_acc, s_rx1, s_s1, s_rx2, s_z, s_res,
     c_q, c_crx, c_acc, c_rx1, c_s1, c_rx2, c_z, c_res,
-    d2, y_hi, y_lo, rest,
+    mt, m2, d2, y2, rest,
     load_sems, send_sems, recv_sems,
 ):
     at_axis = {a: lax.axis_index(a) for a in AXES}
@@ -87,6 +88,7 @@
     z = zh * 2 + zl
     wire = ((at_axis["x"] * ZHI + zh) * SIDE + at_axis["y"]) * 2 + core
     n_wire = SIDE * ZHI * SIDE * 2
+    first_axis, second_axis = ("x", "y"), ("y", "x")
 
     def step(axis, d):
         return {axis: lax.rem(at_axis[axis] + d, SIDE)}
@@ -106,6 +108,10 @@
 
     links = Links(send_sems, recv_sems)
     own = pl.ds(HALO, ROWS)
+
+    def arrived(copies):
+        for copy in copies:
+            copy.wait_recv()
 
     def load(src, dst, i):
         copy = pltpu.make_async_copy(src, dst, load_sems.at[i])
@@ -126,13 +132,17 @@
         pl.semaphore_signal(barrier, inc=1, device_id=where, device_id_type=MESH)
     get_o.wait()
 
-    def turn(src, top):
-        @pl.loop(0, ROWS // 512)
+    @pl.loop(0, ROWS // 512)
+    def _(t):
+        inner = pl.ds(pl.multiple_of(HALO + t * 512, TILE), 512)
+        ot[:COLS, at(t * 512, 512)] = o_m[inner, :].T
+
+    def turn_half(half):
+        @pl.loop(0, 2)
         def _(t):
-            inner = pl.ds(pl.multiple_of(HALO + t * 512, TILE), 512)
-            ot[top : top + COLS, at(t * 512, 512)] = src[inner, :].T
-
-    turn(o_m, 0)
+            start = half * 1024 + t * 512
+            inner = pl.ds(pl.multiple_of(HALO + start, TILE), 512)
+            ot[COLS:, at(start, 512)] = o_o[inner, :].T
 
     def coupling(dst, j, k_start):
         dst[:, j * 512 : (j + 1) * 512] = mm(ot[:COLS, :], pr[:, at(k_start + j * 512, 512)])
@@ -144,6 +154,10 @@
     def core_send(j):
         part = pl.ds(j * 512, 512)
         return links.send(core_tx.at[:, part], core_rx.at[:, part], core=other)
+
+    def swap(start, size):
+        part = pl.ds(pl.multiple_of(HALO + start, TILE), size)
+        return links.send(o_m.at[part, :], o_o.at[part, :], zl=1 - zl)
 
     last, first = pl.ds(ROWS, HALO), pl.ds(HALO, HALO)
     before, after = pl.ds(0, HALO), pl.ds(HALO + ROWS, HALO)
@@ -152,7 +166,8 @@
         links.send(o_m.at[last, :], o_m.at[before, :], **on_wire(1)),
         links.send(o_m.at[first, :], o_m.at[after, :], **on_wire(-1)),
     ]
-    swap = links.send(o_m.at[own, :], o_o.at[own, :], zl=1 - zl)
+    swap_half = swap((1 - zl) * 1024, 1024)
+    swap_early = swap(zl * 1024, EARLY)
     get_pr[1].wait()
     coupling(core_tx, 1, other * HALF)
     to_core.append(core_send(1))
@@ -162,7 +177,6 @@
     get_h = load(ham, hv, 5)
     get_pl = load(phase_l, plv, 6)
 
-    first_axis, second_axis = ("x", "y"), ("y", "x")
     got1 = []
     for lane in range(LANES):
         part = pl.ds(lane * 512, 512)
@@ -180,8 +194,7 @@
     got2 = []
     for lane in range(LANES):
         axis = second_axis[lane]
-        for copy in got1[lane]:
-            copy.wait_recv()
+        arrived(got1[lane])
         mine = acc[:, at(lane * 512 + at_axis[first_axis[lane]] * BLK, BLK)]
         s1[lane] = (mine + rx1[lane, 0]) + (rx1[lane, 1] + rx1[lane, 2])
         got2.append([
@@ -192,47 +205,8 @@
             )
             for d in (1, 2, 3)
         ])
-    got3 = []
-    for lane in range(LANES):
-        for copy in got2[lane]:
-            copy.wait_recv()
-        mine = s1[lane, at(at_axis[second_axis[lane]] * 64, 64), :]
-        s2[lane] = (mine + rx2[lane, 0]) + (rx2[lane, 1] + rx2[lane, 2])
-        got3.append([
-            links.send(
-                s2.at[lane, at(lax.rem(zh + d, ZHI) * 16, 16), :],
-                rx3.at[lane, d - 1],
-                **step("zh", d),
-            )
-            for d in (1, 2, 3)
-        ])
-
-    def k_cols(lane):
-        return at(core * HALF + lane * 512 + at_axis[first_axis[lane]] * BLK, BLK)
-
-    def c_rows(lane):
-        return at(at_axis[second_axis[lane]] * 64, 64)
-
-    got4 = []
-    for lane in range(LANES):
-        for copy in got3[lane]:
-            copy.wait_recv()
-        mine = s2[lane, at(zh * 16, 16), :]
-        piece = (mine + rx3[lane, 0]) + (rx3[lane, 1] + rx3[lane, 2])
-        rows = at(at_axis[second_axis[lane]] * 64 + zh * 16, 16)
-        ct[0, rows, k_cols(lane)] = piece.astype(BF16)
-        got4.append([
-            links.send(ct.at[0, rows, k_cols(lane)], ct.at[d % 2, rows, k_cols(lane)], **along_z(d))
-            for d in range(1, ZALL)
-        ])
-    got5 = []
-    for lane in range(LANES):
-        for copy in got4[lane]:
-            copy.wait_recv()
-        block = ct.at[:, c_rows(lane), k_cols(lane)]
-        got5.append([links.send(block, block, **step(second_axis[lane], d)) for d in (1, 2, 3)])
-
-    def summed(q, crx, part_acc, rx_a, sum_a, rx_b, z_b, res):
+
+    def summed(q, crx, part_acc, rx_a, sum_a, rx_b, z_b, res, both):
         mine_cols, other_cols = at(core * BLK, BLK), at(other * BLK, BLK)
         copy = links.send(q.at[:, other_cols], crx, core=other)
         yield
@@ -252,8 +226,7 @@
         yield
         got_b = []
         for lane in range(LANES):
-            for copy in got[lane]:
-                copy.wait_recv()
+            arrived(got[lane])
             mine = part_acc[at(lane * 256 + at_axis[first_axis[lane]] * 64, 64), :]
             sum_a[lane] = (mine + rx_a[lane, 0]) + (rx_a[lane, 1] + rx_a[lane, 2])
             axis = second_axis[lane]
@@ -268,58 +241,108 @@
         yield
         got_z = []
         for lane in range(LANES):
-            for copy in got_b[lane]:
-                copy.wait_recv()
+            arrived(got_b[lane])
             mine = sum_a[lane, at(at_axis[second_axis[lane]] * 16, 16), :]
-            z_b[lane, zh] = (mine + rx_b[lane, 0]) + (rx_b[lane, 1] + rx_b[lane, 2])
-            got_z.append([links.send(z_b.at[lane, zh], z_b.at[lane, zh], **step("zh", d)) for d in (1, 2, 3)])
+            slot = z if both and lane else zh
+            z_b[lane, slot] = (mine + rx_b[lane, 0]) + (rx_b[lane, 1] + rx_b[lane, 2])
+            if both and lane:
+                places = [along_z(d) for d in range(1, ZALL)]
+            else:
+                places = [step("zh", d) for d in (1, 2, 3)]
+            got_z.append([links.send(z_b.at[lane, slot], z_b.at[lane, slot], **where) for where in places])
         yield
         got_g = []
         for lane in range(LANES):
-            for copy in got_z[lane]:
-                copy.wait_recv()
+            arrived(got_z[lane])
             rows = at(lane * 256 + at_axis[first_axis[lane]] * 64 + at_axis[second_axis[lane]] * 16, 16)
-            res[rows, mine_cols] = (z_b[lane, 0] + z_b[lane, 1]) + (z_b[lane, 2] + z_b[lane, 3])
+            total = (z_b[lane, 0] + z_b[lane, 1]) + (z_b[lane, 2] + z_b[lane, 3])
+            if both and lane:
+                total = total + ((z_b[lane, 4] + z_b[lane, 5]) + (z_b[lane, 6] + z_b[lane, 7]))
+            res[rows, mine_cols] = total
             block = res.at[rows, mine_cols]
             got_g.append([links.send(block, block, **step(second_axis[lane], d)) for d in (1, 2, 3)])
         yield
         got_h = []
         for lane in range(LANES):
-            for copy in got_g[lane]:
-                copy.wait_recv()
+            arrived(got_g[lane])
             block = res.at[at(lane * 256 + at_axis[first_axis[lane]] * 64, 64), mine_cols]
             got_h.append([links.send(block, block, **step(first_axis[lane], d)) for d in (1, 2, 3)])
         yield
         for lane in range(LANES):
-            for copy in got_h[lane]:
-                copy.wait_recv()
+            arrived(got_h[lane])
         block = res.at[:, mine_cols]
         copy = links.send(block, block, core=other)
         yield
         copy.wait_recv()
         yield
 
-    got6 = []
+    swap_half.wait_recv()
+    turn_half(zl)
+    s_q[:COLS, :] = mm(ot[:COLS, :], o_m[own, :])
+    half = pl.ds(pl.multiple_of(HALO + zl * 1024, TILE), 1024)
+    ones = jnp.where(zl == 0, o_o[half, :], o_m[half, :])
+    s_q[COLS:, :] = mm(ot[at(zl * COLS, COLS), at(zl * 1024, 1024)], ones)
+    s_sum = summed(s_q, s_crx, s_acc, s_rx1, s_s1, s_rx2, s_z, s_res, True)
+    next(s_sum)
+
+    got3 = []
     for lane in range(LANES):
-        for copy in got5[lane]:
-            copy.wait_recv()
-        block = ct.at[:, :, k_cols(lane)]
-        got6.append([links.send(block, block, **step(first_axis[lane], d)) for d in (1, 2, 3)])
-
-    swap.wait_recv()
-    put_o = load(o_o.at[own, :], cols_o, 7)
-    halo_o = [
-        links.send(o_o.at[last, :], o_o.at[before, :], **on_wire(1)),
-        links.send(o_o.at[first, :], o_o.at[after, :], **on_wire(-1)),
-    ]
-    turn(o_o, COLS)
-    s_q[...] = mm(ot[...], o_m[own, :])
-    s_sum = summed(s_q, s_crx, s_acc, s_rx1, s_s1, s_rx2, s_z, s_res)
-    next(s_sum)
+        arrived(got2[lane])
+        mine = s1[lane, at(at_axis[second_axis[lane]] * 64, 64), :]
+        s2[lane] = (mine + rx2[lane, 0]) + (rx2[lane, 1] + rx2[lane, 2])
+        got3.append([
+            links.send(
+                s2.at[lane, at(lax.rem(zh + d, ZHI) * 16, 16), :],
+                rx3.at[lane, d - 1],
+                **step("zh", d),
+            )
+            for d in (1, 2, 3)
+        ])
+    next(s_sum)
+
+    def k_cols(lane):
+        return at(core * HALF + lane * 512 + at_axis[first_axis[lane]] * BLK, BLK)
+
+    def c_rows(lane):
+        return at(at_axis[second_axis[lane]] * 64, 64)
+
+    got4 = []
+    for lane in range(LANES):
+        arrived(got3[lane])
+        mine = s2[lane, at(zh * 16, 16), :]
+        piece = (mine + rx3[lane, 0]) + (rx3[lane, 1] + rx3[lane, 2])
+        rows = at(at_axis[second_axis[lane]] * 64 + zh * 16, 16)
+        ct[0, rows, k_cols(lane)] = piece.astype(BF16)
+        got4.append({
+            d: links.send(ct.at[0, rows, k_cols(lane)], ct.at[d % 2, rows, k_cols(lane)], **along_z(d))
+            for d in (2, 4, 6, 1, 3, 5, 7)
+        })
+    next(s_sum)
+    got5 = [[], []]
+
+    def gather_second(side):
+        for lane in range(LANES):
+            arrived([got4[lane][d] for d in range(1, ZALL) if d % 2 == side])
+            block = ct.at[side, c_rows(lane), k_cols(lane)]
+            got5[side].append([links.send(block, block, **step(second_axis[lane], d)) for d in (1, 2, 3)])
+
+    gather_second(0)
+    next(s_sum)
+    got6 = [[], []]
+
+    def gather_first(side):
+        for lane in range(LANES):
+            arrived(got5[side][lane])
+            block = ct.at[side, :, k_cols(lane)]
+            got6[side].append([links.send(block, block, **step(first_axis[lane], d)) for d in (1, 2, 3)])
+
+    gather_first(0)
+    gather_second(1)
+    next(s_sum)
+    swap_late = swap(zl * 1024 + EARLY, LATE)
 
     get_h.wait()
-    for copy in halo:
-        copy.wait_recv()
+    arrived(halo)
 
     @pl.loop(0, ROWS // BLK)
     def _(i):
@@ -329,13 +352,16 @@
             total = total + mm(hv[i, s], pick(blocks, off[s, i]))
         image[at(i * BLK, BLK), :] = total
 
-    next(s_sum)
-    got7 = []
-    for lane in range(LANES):
-        for copy in got6[lane]:
-            copy.wait_recv()
-        block = ct.at[:, :, at(core * HALF + lane * 512, 512)]
-        got7.append(links.send(block, block, core=other))
+    got7 = [[], []]
+
+    def gather_core(side):
+        for lane in range(LANES):
+            arrived(got6[side][lane])
+            block = ct.at[side, :, at(core * HALF + lane * 512, 512)]
+            got7[side].append(links.send(block, block, core=other))
+
+    gather_core(0)
+    gather_first(1)
     next(s_sum)
     get_pl.wait()
 
@@ -346,76 +372,77 @@
         rows = at(t * 1024, 1024)
         image[rows, :] += mm_nt(plv[rows, k_mine], ct[0, :, k_mine])
 
-    for copy in got7:
-        copy.wait_recv()
+    arrived(got7[0])
 
     @pl.loop(0, ROWS // 1024)
     def _(t):
         rows = at(t * 1024, 1024)
         im_hi[rows, :], im_lo[rows, :] = split(image[rows, :] + mm_nt(plv[rows, k_other], ct[0, :, k_other]))
 
+    next(s_sum)
+    gather_core(1)
+    arrived([swap_early, swap_late])
+    turn_half(1 - zl)
     c_q[...] = mm(ot[...], im_hi[...]) + mm(ot[...], im_lo[...])
-    c_sum = summed(c_q, c_crx, c_acc, c_rx1, c_s1, c_rx2, c_z, c_res)
-    next(c_sum)
-    next(s_sum)
-    next(c_sum)
-    next(s_sum)
-    next(c_sum)
-    next(s_sum)
-    next(c_sum)
-    next(s_sum)
-    next(s_sum)
-
+    c_sum = summed(c_q, c_crx, c_acc, c_rx1, c_s1, c_rx2, c_z, c_res, False)
+    next(c_sum)
+    halo_o = [
+        links.send(o_o.at[last, :], o_o.at[before, :], **on_wire(1)),
+        links.send(o_o.at[first, :], o_o.at[after, :], **on_wire(-1)),
+    ]
+    put_o = load(o_o.at[own, :], cols_o, 7)
+
+    next(s_sum)
     scale = 1.0 / TOTAL
     row = lax.broadcasted_iota(jnp.int32, (COLS, COLS), 0)
     col = lax.broadcasted_iota(jnp.int32, (COLS, COLS), 1)
     m_m = jnp.where(row == col, 2.0, 0.0) - s_res[:COLS, :] * scale
-    m_o = 0.0 - s_res[COLS:, :] * scale
-    mm_hi, mm_lo = split(m_m)
-    mo_hi, mo_lo = split(m_o)
-    tm_hi, tm_lo = split(m_m.T)
-    to_hi, to_lo = split(m_o.T)
+    s_01 = 0.0 - s_res[COLS:, :] * scale
+    s_10 = s_01.T
+    m_o = jnp.where(zl == 1, s_01, s_10)
+    m2[0, :, :COLS], m2[0, :, COLS:] = split(m_m)
+    m2[1, :, :COLS], m2[1, :, COLS:] = split(m_o)
+    mt[:COLS, :COLS], mt[COLS:, :COLS] = split(m_m.T)
+    mt[:COLS, COLS:], mt[COLS:, COLS:] = split(jnp.where(zl == 1, s_10, s_01))
+    next(c_sum)
+    arrived(got7[1])
 
     @pl.loop(0, KDIM // 512)
     def _(t):
         cols = at(t * 512, 512)
-        a, b = ct[0, :, cols], ct[1, :, cols]
-        d = (mm(tm_hi, a) + mm(to_hi, b)) + (mm(tm_lo, a) + mm(to_lo, b))
-        d2[:COLS, cols], d2[COLS:, cols] = split(d)
-
-    next(c_sum)
-    for copy in halo_o:
-        copy.wait_recv()
+        both = mm(mt[:, :COLS], ct[0, :, cols]) + mm(mt[:, COLS:], ct[1, :, cols])
+        d2[:COLS, cols], d2[COLS:, cols] = split(both[:COLS, :] + both[COLS:, :])
+
+    next(c_sum)
+    arrived(halo_o)
 
     @pl.loop(0, (ROWS + 2 * HALO) // 512)
     def _(t):
         rows = at(t * 512, 512)
-        a, b = o_m[rows, :], o_o[rows, :]
-        y = (mm(a, mm_hi) + mm(b, mo_hi)) + (mm(a, mm_lo) + mm(b, mo_lo))
-        y_hi[rows, :], y_lo[rows, :] = split(y)
+        both = mm(o_m[rows, :], m2[0]) + mm(o_o[rows, :], m2[1])
+        y2[rows, :COLS], y2[rows, COLS:] = split(both[:, :COLS] + both[:, COLS:])
 
     next(c_sum)
 
     @pl.loop(0, ROWS // BLK)
     def _(i):
-        total = None
-        for src in (y_lo, y_hi):
-            blocks = near(src, i)
-            term = mm(hv[i, 0], blocks[2])
-            for s in (1, 2):
-                term = term + mm(hv[i, s], pick(blocks, off[s, i]))
-            total = term if total is None else total + term
-        rest[at(i * BLK, BLK), :] = total
-
-    next(c_sum)
-
-    @pl.loop(0, ROWS // 512)
-    def _(t):
-        rows = at(t * 512, 512)
+        blocks = near(y2, i)
+        both = mm(hv[i, 0], blocks[2])
+        for s in (1, 2):
+            both = both + mm(hv[i, s], pick(blocks, off[s, i]))
+        rest[at(i * BLK, BLK), :] = both[:, :COLS] + both[:, COLS:]
+
+    def with_left(t):
+        rows = pl.ds(t * 1024, 1024)
         both = mm_nt(plv[rows, :], d2[...])
         rest[rows, :] += both[:, :COLS] + both[:, COLS:]
 
+    with_left(0)
+    next(c_sum)
+    with_left(1)
     put_base = load(rest, base, 8)
+    next(c_sum)
+    next(c_sum)
     next(c_sum)
     put_cross = load(c_res, cross, 9)
     for copy in (put_o, put_base, put_cross):
@@ -434,7 +461,7 @@
 
 
 def body(hamiltonian, offsets, phase_left, phase_right, orbitals):
-    def sums():
+    def sums(depth):
         return [
             pltpu.VMEM((512, 256), F32),
             pltpu.VMEM((512, 128), F32),
@@ -442,7 +469,7 @@
             pltpu.VMEM((2, 3, 64, 128), F32),
             pltpu.VMEM((2, 64, 128), F32),
             pltpu.VMEM((2, 3, 16, 128), F32),
-            pltpu.VMEM((2, 4, 16, 128), F32),
+            pltpu.VMEM((2, depth, 16, 128), F32),
             pltpu.VMEM((512, 256), F32),
         ]
 
@@ -475,11 +502,12 @@
             pltpu.VMEM((ROWS, COLS), F32),
             pltpu.VMEM((ROWS, COLS), BF16),
             pltpu.VMEM((ROWS, COLS), BF16),
-            *sums(),
-            *sums(),
+            *sums(ZALL),
+            *sums(ZHI),
+            pltpu.VMEM((2 * COLS, 2 * COLS), BF16),
+            pltpu.VMEM((2, COLS, 2 * COLS), BF16),
             pltpu.VMEM((2 * COLS, KDIM), BF16),
-            pltpu.VMEM((ROWS + 2 * HALO, COLS), BF16),
-            pltpu.VMEM((ROWS + 2 * HALO, COLS), BF16),
+            pltpu.VMEM((ROWS + 2 * HALO, 2 * COLS), BF16),
             pltpu.VMEM((ROWS, COLS), F32),
             pltpu.SemaphoreType.DMA((10,)),
             pltpu.SemaphoreType.DMA((N_SEMS,)),
@@ -499,7 +527,7 @@
         in_specs=[tile, tile, tile, whole],
         out_specs=tile,
         scratch_shapes=[pltpu.VMEM((2 * COLS, COLS), BF16), pltpu.VMEM((2 * COLS, COLS), BF16)],
-        compiler_params=pltpu.CompilerParams(vmem_limit_bytes=24 << 20),
+        compiler_params=pltpu.CompilerParams(vmem_limit_bytes=60 << 20),
     )(base, orbitals, cols_o, cross)
 
 

time: 103 us -> 91.5 us (0.89)
  Pallas kernels: 99.4 us -> 91.3 us
  local copies, waits for them, and re-layouts: 3.85 us -> 0 us
    pallas_call x1, Pallas kernels: 96.4 us -> 86 us  [body(): pl.pallas_call(kernel, out_shape=[jax.ShapeDtypeStruct((ROWS, COLS), F32)...]
    unnamed x8 -> x0, local copies, waits for them, and re-layouts: 3.85 us -> none
    pallas_call x1, Pallas kernels: 3.05 us -> 5.32 us  [body(): pl.pallas_call(last_kernel, grid=(ROWS // 512,), out_shape=jax.ShapeDtype...]
where the time goes in v3:
time: 91.5 us; the launch traced here: 91.3 us
  Pallas kernels  91.3 us (100%)
    pallas_call x1, Pallas kernels, body(): pl.pallas_call(kernel, out_shape=[jax.ShapeDtypeStruct((ROWS, COLS), F32)...  86 us
    pallas_call x1, Pallas kernels, body(): pl.pallas_call(last_kernel, grid=(ROWS // 512,), out_shape=jax.ShapeDtype...  5.32 us

profile of v3, /device:TPU:1, one launch (start us, length us, event | category | flops | bytes accessed | tf_op | source)
XLA Modules:
  0.0 91.3 jit_solution(178887931900523364)
XLA Ops:
  0.0 86.0 %shard_map.55 = (f32[2048,256]{1,0:T(8,128)}, bf16[2048,256]{1,0:T(8,128)(2,1)}, f32[512,256]{1,0:T(8,128)}) custom-call(bf16[16,3,128,128]{3,2,1,0:T(8,128)(2,1)} %ham.1, s32[3,16]{1,0:T(4,128)} %bitcast.1, bf16[2048,2048]{1,0:T(8,128)(2,1)} %phase_l.1, bf16[2048,2048]{1,0:T(8,128)(2,1)} %phase_r.1, bf16[2048,256]{1,0:T(8,128)(2,1)} %o_m.1), custom_call_target="tpu_custom_call" | custom-call | flops 16000000000 | bytes 20971520 | tf_op jit(solution)/shard_map/pallas_call | solution.py:477
  86.0 5.3 %shard_map.56 = f32[2048,256]{1,0:T(8,128)} custom-call(f32[2048,256]{1,0:T(8,128)} %get-tuple-element.8.base, bf16[2048,256]{1,0:T(8,128)(2,1)} %o_m.1, bf16[2048,256]{1,0:T(8,128)(2,1)} %get-tuple-element.9.o_o, f32[512,256]{1,0:T(8,128)} %get-tuple-element.10.cross), custom_call_target="tpu_custom_call" | custom-call | tf_op jit(solution)/shard_map/pallas_call | solution.py:523

commit v4 on v3

--- a/solution.py
+++ b/solution.py
@@ -37,6 +37,12 @@
 
 def near(src, i):
     return [src[at((i + r) * BLK, BLK), :] for r in range(5)]
+
+
+def banded(h, blocks, shifts):
+    left = jnp.concatenate([h[0], h[1], h[2]], axis=1)
+    right = jnp.concatenate([blocks[2], pick(blocks, shifts[0]), pick(blocks, shifts[1])], axis=0)
+    return mm(left, right)
 
 
 def pick(blocks, shift):
@@ -131,6 +137,20 @@
     for where in greeted:
         pl.semaphore_signal(barrier, inc=1, device_id=where, device_id_type=MESH)
     get_o.wait()
+    pl.semaphore_wait(barrier, len(greeted))
+
+    def swap(start, size):
+        part = pl.ds(pl.multiple_of(HALO + start, TILE), size)
+        return links.send(o_m.at[part, :], o_o.at[part, :], zl=1 - zl)
+
+    last, first = pl.ds(ROWS, HALO), pl.ds(HALO, HALO)
+    before, after = pl.ds(0, HALO), pl.ds(HALO + ROWS, HALO)
+    halo = [
+        links.send(o_m.at[last, :], o_m.at[before, :], **on_wire(1)),
+        links.send(o_m.at[first, :], o_m.at[after, :], **on_wire(-1)),
+    ]
+    swap_half = swap((1 - zl) * 1024, 1024)
+    swap_early = swap(zl * 1024, EARLY)
 
     @pl.loop(0, ROWS // 512)
     def _(t):
@@ -147,30 +167,12 @@
     def coupling(dst, j, k_start):
         dst[:, j * 512 : (j + 1) * 512] = mm(ot[:COLS, :], pr[:, at(k_start + j * 512, 512)])
 
-    get_pr[0].wait()
-    coupling(core_tx, 0, other * HALF)
-    pl.semaphore_wait(barrier, len(greeted))
-
-    def core_send(j):
+    to_core = []
+    for j in range(2):
+        get_pr[j].wait()
+        coupling(core_tx, j, other * HALF)
         part = pl.ds(j * 512, 512)
-        return links.send(core_tx.at[:, part], core_rx.at[:, part], core=other)
-
-    def swap(start, size):
-        part = pl.ds(pl.multiple_of(HALO + start, TILE), size)
-        return links.send(o_m.at[part, :], o_o.at[part, :], zl=1 - zl)
-
-    last, first = pl.ds(ROWS, HALO), pl.ds(HALO, HALO)
-    before, after = pl.ds(0, HALO), pl.ds(HALO + ROWS, HALO)
-    to_core = [core_send(0)]
-    halo = [
-        links.send(o_m.at[last, :], o_m.at[before, :], **on_wire(1)),
-        links.send(o_m.at[first, :], o_m.at[after, :], **on_wire(-1)),
-    ]
-    swap_half = swap((1 - zl) * 1024, 1024)
-    swap_early = swap(zl * 1024, EARLY)
-    get_pr[1].wait()
-    coupling(core_tx, 1, other * HALF)
-    to_core.append(core_send(1))
+        to_core.append(links.send(core_tx.at[:, part], core_rx.at[:, part], core=other))
     for j in range(2):
         get_pr[2 + j].wait()
         coupling(acc, j, core * HALF)
@@ -346,11 +348,7 @@
 
     @pl.loop(0, ROWS // BLK)
     def _(i):
-        blocks = near(o_m, i)
-        total = mm(hv[i, 0], blocks[2])
-        for s in (1, 2):
-            total = total + mm(hv[i, s], pick(blocks, off[s, i]))
-        image[at(i * BLK, BLK), :] = total
+        image[at(i * BLK, BLK), :] = banded(hv[i], near(o_m, i), (off[1, i], off[2, i]))
 
     got7 = [[], []]
 
@@ -426,11 +424,10 @@
 
     @pl.loop(0, ROWS // BLK)
     def _(i):
-        blocks = near(y2, i)
-        both = mm(hv[i, 0], blocks[2])
-        for s in (1, 2):
-            both = both + mm(hv[i, s], pick(blocks, off[s, i]))
+        both = banded(hv[i], near(y2, i), (off[1, i], off[2, i]))
         rest[at(i * BLK, BLK), :] = both[:, :COLS] + both[:, COLS:]
+
+    next(c_sum)
 
     def with_left(t):
         rows = pl.ds(t * 1024, 1024)
@@ -441,7 +438,6 @@
     next(c_sum)
     with_left(1)
     put_base = load(rest, base, 8)
-    next(c_sum)
     next(c_sum)
     next(c_sum)
     put_cross = load(c_res, cross, 9)

time: 91.5 us -> 89.2 us (0.975)
  Pallas kernels: 91.3 us -> 89 us
    pallas_call x1, Pallas kernels: 86 us -> 83.7 us  [body(): pl.pallas_call(kernel, out_shape=[jax.ShapeDtypeStruct((ROWS, COLS), F32)...]
where the time goes in v4:
time: 89.2 us; the launch traced here: 89 us
  Pallas kernels  89 us (100%)
    pallas_call x1, Pallas kernels, body(): pl.pallas_call(kernel, out_shape=[jax.ShapeDtypeStruct((ROWS, COLS), F32)...  83.7 us
    pallas_call x1, Pallas kernels, body(): pl.pallas_call(last_kernel, grid=(ROWS // 512,), out_shape=jax.ShapeDtype...  5.32 us

profile of v4, /device:TPU:1, one launch (start us, length us, event | category | flops | bytes accessed | tf_op | source)
XLA Modules:
  0.0 89.0 jit_solution(591212473146779771)
XLA Ops:
  0.0 83.7 %shard_map.55 = (f32[2048,256]{1,0:T(8,128)}, bf16[2048,256]{1,0:T(8,128)(2,1)}, f32[512,256]{1,0:T(8,128)}) custom-call(bf16[16,3,128,128]{3,2,1,0:T(8,128)(2,1)} %ham.1, s32[3,16]{1,0:T(4,128)} %bitcast.1, bf16[2048,2048]{1,0:T(8,128)(2,1)} %phase_l.1, bf16[2048,2048]{1,0:T(8,128)(2,1)} %phase_r.1, bf16[2048,256]{1,0:T(8,128)(2,1)} %o_m.1), custom_call_target="tpu_custom_call" | custom-call | flops 16000000000 | bytes 20971520 | tf_op jit(solution)/shard_map/pallas_call | solution.py:473
  83.7 5.3 %shard_map.56 = f32[2048,256]{1,0:T(8,128)} custom-call(f32[2048,256]{1,0:T(8,128)} %get-tuple-element.8.base, bf16[2048,256]{1,0:T(8,128)(2,1)} %o_m.1, bf16[2048,256]{1,0:T(8,128)(2,1)} %get-tuple-element.9.o_o, f32[512,256]{1,0:T(8,128)} %get-tuple-element.10.cross), custom_call_target="tpu_custom_call" | custom-call | tf_op jit(solution)/shard_map/pallas_call | solution.py:519

commit v5 on v4

--- a/solution.py
+++ b/solution.py
@@ -75,14 +75,14 @@
             copy.wait_send()
 
 
-N_SEMS = 160
+N_SEMS = 140
 EARLY, LATE = 256, 768
 
 
 def kernel(
     ham, off, phase_l, phase_r, orb, base, cols_o, cross,
     o_m, o_o, ot, pr, plv, hv,
-    core_tx, core_rx, acc, rx1, s1, rx2, s2, rx3, ct, image, im_hi, im_lo,
+    core_tx, core_rx, acc, rx1, s1, rx2, s2, rx3, ct, b_hi, b_lo, g_o, g_hi, g_lo,
     s_q, s_crx, s_acc, s_rx1, s_s1, s_rx2, s_z, s_res,
     c_q, c_crx, c_acc, c_rx1, c_s1, c_rx2, c_z, c_res,
     mt, m2, d2, y2, rest,
@@ -193,6 +193,13 @@
             )
             for d in (1, 2, 3)
         ])
+    get_pl.wait()
+
+    @pl.loop(0, KDIM // 512)
+    def _(t):
+        cols = at(t * 512, 512)
+        g_hi[:COLS, cols], g_lo[:COLS, cols] = split(mm(ot[:COLS, :], plv[:, cols]))
+
     got2 = []
     for lane in range(LANES):
         axis = second_axis[lane]
@@ -301,6 +308,13 @@
             for d in (1, 2, 3)
         ])
     next(s_sum)
+    half_a, half_b = at(zl * 1024, 1024), at((1 - zl) * 1024, 1024)
+
+    @pl.loop(0, KDIM // 512)
+    def _(t):
+        cols = at(t * 512, 512)
+        g_o[:, cols] = mm(ot[COLS:, half_a], plv[half_a, cols])
+
 
     def k_cols(lane):
         return at(core * HALF + lane * 512 + at_axis[first_axis[lane]] * BLK, BLK)
@@ -320,6 +334,14 @@
             for d in (2, 4, 6, 1, 3, 5, 7)
         })
     next(s_sum)
+    get_h.wait()
+    arrived(halo)
+
+    @pl.loop(0, ROWS // BLK)
+    def _(i):
+        rows = at(i * BLK, BLK)
+        b_hi[rows, :], b_lo[rows, :] = split(banded(hv[i], near(o_m, i), (off[1, i], off[2, i])))
+
     got5 = [[], []]
 
     def gather_second(side):
@@ -330,6 +352,9 @@
 
     gather_second(0)
     next(s_sum)
+    swap_late = swap(zl * 1024 + EARLY, LATE)
+    c_q[:COLS, :] = mm(ot[:COLS, :], b_hi[...]) + mm(ot[:COLS, :], b_lo[...])
+    c_q[COLS:, :] = mm(ot[COLS:, half_a], b_hi[half_a, :]) + mm(ot[COLS:, half_a], b_lo[half_a, :])
     got6 = [[], []]
 
     def gather_first(side):
@@ -340,15 +365,6 @@
 
     gather_first(0)
     gather_second(1)
-    next(s_sum)
-    swap_late = swap(zl * 1024 + EARLY, LATE)
-
-    get_h.wait()
-    arrived(halo)
-
-    @pl.loop(0, ROWS // BLK)
-    def _(i):
-        image[at(i * BLK, BLK), :] = banded(hv[i], near(o_m, i), (off[1, i], off[2, i]))
 
     got7 = [[], []]
 
@@ -360,28 +376,23 @@
 
     gather_core(0)
     gather_first(1)
-    next(s_sum)
-    get_pl.wait()
-
-    k_mine, k_other = at(core * HALF, HALF), at(other * HALF, HALF)
-
-    @pl.loop(0, ROWS // 1024)
-    def _(t):
-        rows = at(t * 1024, 1024)
-        image[rows, :] += mm_nt(plv[rows, k_mine], ct[0, :, k_mine])
-
-    arrived(got7[0])
-
-    @pl.loop(0, ROWS // 1024)
-    def _(t):
-        rows = at(t * 1024, 1024)
-        im_hi[rows, :], im_lo[rows, :] = split(image[rows, :] + mm_nt(plv[rows, k_other], ct[0, :, k_other]))
-
-    next(s_sum)
-    gather_core(1)
     arrived([swap_early, swap_late])
     turn_half(1 - zl)
-    c_q[...] = mm(ot[...], im_hi[...]) + mm(ot[...], im_lo[...])
+
+    @pl.loop(0, KDIM // 512)
+    def _(t):
+        cols = at(t * 512, 512)
+        g_hi[COLS:, cols], g_lo[COLS:, cols] = split(g_o[:, cols] + mm(ot[COLS:, half_b], plv[half_b, cols]))
+
+    c_q[COLS:, :] += mm(ot[COLS:, half_b], b_hi[half_b, :]) + mm(ot[COLS:, half_b], b_lo[half_b, :])
+    next(s_sum)
+
+    def with_coupling(k):
+        c_q[...] += mm_nt(g_hi[:, k], ct[0, :, k]) + mm_nt(g_lo[:, k], ct[0, :, k])
+
+    with_coupling(at(core * HALF, HALF))
+    arrived(got7[0])
+    with_coupling(at(other * HALF, HALF))
     c_sum = summed(c_q, c_crx, c_acc, c_rx1, c_s1, c_rx2, c_z, c_res, False)
     next(c_sum)
     halo_o = [
@@ -389,8 +400,13 @@
         links.send(o_o.at[first, :], o_o.at[after, :], **on_wire(-1)),
     ]
     put_o = load(o_o.at[own, :], cols_o, 7)
-
-    next(s_sum)
+    gather_core(1)
+    next(s_sum)
+    next(c_sum)
+    next(s_sum)
+    next(c_sum)
+    next(s_sum)
+
     scale = 1.0 / TOTAL
     row = lax.broadcasted_iota(jnp.int32, (COLS, COLS), 0)
     col = lax.broadcasted_iota(jnp.int32, (COLS, COLS), 1)
@@ -402,7 +418,6 @@
     m2[1, :, :COLS], m2[1, :, COLS:] = split(m_o)
     mt[:COLS, :COLS], mt[COLS:, :COLS] = split(m_m.T)
     mt[:COLS, COLS:], mt[COLS:, COLS:] = split(jnp.where(zl == 1, s_10, s_01))
-    next(c_sum)
     arrived(got7[1])
 
     @pl.loop(0, KDIM // 512)
@@ -420,8 +435,6 @@
         both = mm(o_m[rows, :], m2[0]) + mm(o_o[rows, :], m2[1])
         y2[rows, :COLS], y2[rows, COLS:] = split(both[:, :COLS] + both[:, COLS:])
 
-    next(c_sum)
-
     @pl.loop(0, ROWS // BLK)
     def _(i):
         both = banded(hv[i], near(y2, i), (off[1, i], off[2, i]))
@@ -446,14 +459,13 @@
     links.finish()
 
 
-def last_kernel(base, o_m, o_o, cross, out, x_hi, x_lo):
+def last_kernel(base, o_m, o_o, cross, out, x2):
     @pl.when(pl.program_id(0) == 0)
     def _():
-        x_hi[...], x_lo[...] = split(cross[...] * (1.0 / TOTAL))
-
-    a, b = o_m[...], o_o[...]
-    low = mm(a, x_lo[:COLS, :]) + mm(b, x_lo[COLS:, :])
-    out[...] = base[...] - ((mm(a, x_hi[:COLS, :]) + mm(b, x_hi[COLS:, :])) + low)
+        x2[:, :COLS], x2[:, COLS:] = split(cross[...] * (1.0 / TOTAL))
+
+    both = mm(o_m[...], x2[:COLS, :]) + mm(o_o[...], x2[COLS:, :])
+    out[...] = base[...] - (both[:, :COLS] + both[:, COLS:])
 
 
 def body(hamiltonian, offsets, phase_left, phase_right, orbitals):
@@ -495,9 +507,11 @@
             pltpu.VMEM((2, 64, 128), F32),
             pltpu.VMEM((2, 3, 16, 128), F32),
             pltpu.VMEM((2, COLS, KDIM), BF16),
-            pltpu.VMEM((ROWS, COLS), F32),
             pltpu.VMEM((ROWS, COLS), BF16),
             pltpu.VMEM((ROWS, COLS), BF16),
+            pltpu.VMEM((COLS, KDIM), F32),
+            pltpu.VMEM((2 * COLS, KDIM), BF16),
+            pltpu.VMEM((2 * COLS, KDIM), BF16),
             *sums(ZALL),
             *sums(ZHI),
             pltpu.VMEM((2 * COLS, 2 * COLS), BF16),
@@ -522,7 +536,7 @@
         out_shape=jax.ShapeDtypeStruct((ROWS, COLS), F32),
         in_specs=[tile, tile, tile, whole],
         out_specs=tile,
-        scratch_shapes=[pltpu.VMEM((2 * COLS, COLS), BF16), pltpu.VMEM((2 * COLS, COLS), BF16)],
+        scratch_shapes=[pltpu.VMEM((2 * COLS, 2 * COLS), BF16)],
         compiler_params=pltpu.CompilerParams(vmem_limit_bytes=60 << 20),
     )(base, orbitals, cols_o, cross)
 

time: 89.2 us -> 89.9 us (level)
  no operation moved by 1% of the time
where the time goes in v5:
time: 89.9 us; the launch traced here: 89.7 us
  Pallas kernels  89.7 us (100%)
    pallas_call x1, Pallas kernels, body(): pl.pallas_call(kernel, out_shape=[jax.ShapeDtypeStruct((ROWS, COLS), F32)...  84.3 us
    pallas_call x1, Pallas kernels, body(): pl.pallas_call(last_kernel, grid=(ROWS // 512,), out_shape=jax.ShapeDtype...  5.32 us

profile of v5, /device:TPU:1, one launch (start us, length us, event | category | flops | bytes accessed | tf_op | source)
XLA Modules:
  0.0 89.7 jit_solution(8335302064179008901)
XLA Ops:
  0.0 84.3 %shard_map.55 = (f32[2048,256]{1,0:T(8,128)}, bf16[2048,256]{1,0:T(8,128)(2,1)}, f32[512,256]{1,0:T(8,128)}) custom-call(bf16[16,3,128,128]{3,2,1,0:T(8,128)(2,1)} %ham.1, s32[3,16]{1,0:T(4,128)} %bitcast.1, bf16[2048,2048]{1,0:T(8,128)(2,1)} %phase_l.1, bf16[2048,2048]{1,0:T(8,128)(2,1)} %phase_r.1, bf16[2048,256]{1,0:T(8,128)(2,1)} %o_m.1), custom_call_target="tpu_custom_call" | custom-call | flops 16000000000 | bytes 20971520 | tf_op jit(solution)/shard_map/pallas_call | solution.py:485
  84.3 5.3 %shard_map.56 = f32[2048,256]{1,0:T(8,128)} custom-call(f32[2048,256]{1,0:T(8,128)} %get-tuple-element.8.base, bf16[2048,256]{1,0:T(8,128)(2,1)} %o_m.1, bf16[2048,256]{1,0:T(8,128)(2,1)} %get-tuple-element.9.o_o, f32[512,256]{1,0:T(8,128)} %get-tuple-element.10.cross), custom_call_target="tpu_custom_call" | custom-call | tf_op jit(solution)/shard_map/pallas_call | solution.py:533

commit v6 on v5

--- a/solution.py
+++ b/solution.py
@@ -385,7 +385,6 @@
         g_hi[COLS:, cols], g_lo[COLS:, cols] = split(g_o[:, cols] + mm(ot[COLS:, half_b], plv[half_b, cols]))
 
     c_q[COLS:, :] += mm(ot[COLS:, half_b], b_hi[half_b, :]) + mm(ot[COLS:, half_b], b_lo[half_b, :])
-    next(s_sum)
 
     def with_coupling(k):
         c_q[...] += mm_nt(g_hi[:, k], ct[0, :, k]) + mm_nt(g_lo[:, k], ct[0, :, k])
@@ -401,6 +400,8 @@
     ]
     put_o = load(o_o.at[own, :], cols_o, 7)
     gather_core(1)
+    next(s_sum)
+    next(c_sum)
     next(s_sum)
     next(c_sum)
     next(s_sum)
@@ -426,7 +427,6 @@
         both = mm(mt[:, :COLS], ct[0, :, cols]) + mm(mt[:, COLS:], ct[1, :, cols])
         d2[:COLS, cols], d2[COLS:, cols] = split(both[:COLS, :] + both[COLS:, :])
 
-    next(c_sum)
     arrived(halo_o)
 
     @pl.loop(0, (ROWS + 2 * HALO) // 512)
@@ -435,20 +435,20 @@
         both = mm(o_m[rows, :], m2[0]) + mm(o_o[rows, :], m2[1])
         y2[rows, :COLS], y2[rows, COLS:] = split(both[:, :COLS] + both[:, COLS:])
 
+    next(c_sum)
     @pl.loop(0, ROWS // BLK)
     def _(i):
         both = banded(hv[i], near(y2, i), (off[1, i], off[2, i]))
         rest[at(i * BLK, BLK), :] = both[:, :COLS] + both[:, COLS:]
 
-    next(c_sum)
 
     def with_left(t):
         rows = pl.ds(t * 1024, 1024)
         both = mm_nt(plv[rows, :], d2[...])
         rest[rows, :] += both[:, :COLS] + both[:, COLS:]
 
+    next(c_sum)
     with_left(0)
-    next(c_sum)
     with_left(1)
     put_base = load(rest, base, 8)
     next(c_sum)
@@ -528,11 +528,11 @@
         ),
         cost_estimate=pl.CostEstimate(flops=16 * 10**9, bytes_accessed=20 * 2**20, transcendentals=0),
     )(hamiltonian, offsets.T, phase_left, phase_right, orbitals)
-    tile = pl.BlockSpec((512, COLS), lambda i: (i, 0))
+    tile = pl.BlockSpec((1024, COLS), lambda i: (i, 0))
     whole = pl.BlockSpec((2 * COLS, COLS), lambda i: (0, 0))
     return pl.pallas_call(
         last_kernel,
-        grid=(ROWS // 512,),
+        grid=(ROWS // 1024,),
         out_shape=jax.ShapeDtypeStruct((ROWS, COLS), F32),
         in_specs=[tile, tile, tile, whole],
         out_specs=tile,

time: 89.9 us -> 86.1 us (0.958)
  Pallas kernels: 89.7 us -> 85.9 us
    pallas_call x1, Pallas kernels: 84.3 us -> 81.5 us  [body(): pl.pallas_call(kernel, out_shape=[jax.ShapeDtypeStruct((ROWS, COLS), F32)...]
    pallas_call x1, Pallas kernels: 5.32 us -> 4.41 us  [body(): pl.pallas_call(last_kernel, grid=(ROWS // 1024,), out_shape=jax.ShapeDtyp...]
where the time goes in v6:
time: 86.1 us; the launch traced here: 85.9 us
  Pallas kernels  85.9 us (100%)
    pallas_call x1, Pallas kernels, body(): pl.pallas_call(kernel, out_shape=[jax.ShapeDtypeStruct((ROWS, COLS), F32)...  81.5 us
    pallas_call x1, Pallas kernels, body(): pl.pallas_call(last_kernel, grid=(ROWS // 1024,), out_shape=jax.ShapeDtyp...  4.41 us

profile of v6, /device:TPU:1, one launch (start us, length us, event | category | flops | bytes accessed | tf_op | source)
XLA Modules:
  0.0 85.9 jit_solution(3345129148023628326)
XLA Ops:
  0.0 81.5 %shard_map.55 = (f32[2048,256]{1,0:T(8,128)}, bf16[2048,256]{1,0:T(8,128)(2,1)}, f32[512,256]{1,0:T(8,128)}) custom-call(bf16[16,3,128,128]{3,2,1,0:T(8,128)(2,1)} %ham.1, s32[3,16]{1,0:T(4,128)} %bitcast.1, bf16[2048,2048]{1,0:T(8,128)(2,1)} %phase_l.1, bf16[2048,2048]{1,0:T(8,128)(2,1)} %phase_r.1, bf16[2048,256]{1,0:T(8,128)(2,1)} %o_m.1), custom_call_target="tpu_custom_call" | custom-call | flops 16000000000 | bytes 20971520 | tf_op jit(solution)/shard_map/pallas_call | solution.py:485
  81.5 4.4 %shard_map.56 = f32[2048,256]{1,0:T(8,128)} custom-call(f32[2048,256]{1,0:T(8,128)} %get-tuple-element.8.base, bf16[2048,256]{1,0:T(8,128)(2,1)} %o_m.1, bf16[2048,256]{1,0:T(8,128)(2,1)} %get-tuple-element.9.o_o, f32[512,256]{1,0:T(8,128)} %get-tuple-element.10.cross), custom_call_target="tpu_custom_call" | custom-call | tf_op jit(solution)/shard_map/pallas_call | solution.py:533

commit v7 on v6

--- a/solution.py
+++ b/solution.py
@@ -376,6 +376,12 @@
 
     gather_core(0)
     gather_first(1)
+    def with_coupling(top):
+        rows = pl.ds(top, COLS)
+        c_q[rows, :] += mm_nt(g_hi[rows, :], ct[0]) + mm_nt(g_lo[rows, :], ct[0])
+
+    arrived(got7[0])
+    with_coupling(0)
     arrived([swap_early, swap_late])
     turn_half(1 - zl)
 
@@ -386,12 +392,7 @@
 
     c_q[COLS:, :] += mm(ot[COLS:, half_b], b_hi[half_b, :]) + mm(ot[COLS:, half_b], b_lo[half_b, :])
 
-    def with_coupling(k):
-        c_q[...] += mm_nt(g_hi[:, k], ct[0, :, k]) + mm_nt(g_lo[:, k], ct[0, :, k])
-
-    with_coupling(at(core * HALF, HALF))
-    arrived(got7[0])
-    with_coupling(at(other * HALF, HALF))
+    with_coupling(COLS)
     c_sum = summed(c_q, c_crx, c_acc, c_rx1, c_s1, c_rx2, c_z, c_res, False)
     next(c_sum)
     halo_o = [

time: 86.1 us -> 84.9 us (0.986)
  Pallas kernels: 85.9 us -> 84.8 us
    pallas_call x1, Pallas kernels: 81.5 us -> 80.3 us  [body(): pl.pallas_call(kernel, out_shape=[jax.ShapeDtypeStruct((ROWS, COLS), F32)...]
where the time goes in v7:
time: 84.9 us; the launch traced here: 84.8 us
  Pallas kernels  84.8 us (100%)
    pallas_call x1, Pallas kernels, body(): pl.pallas_call(kernel, out_shape=[jax.ShapeDtypeStruct((ROWS, COLS), F32)...  80.3 us
    pallas_call x1, Pallas kernels, body(): pl.pallas_call(last_kernel, grid=(ROWS // 1024,), out_shape=jax.ShapeDtyp...  4.41 us

profile of v7, /device:TPU:1, one launch (start us, length us, event | category | flops | bytes accessed | tf_op | source)
XLA Modules:
  0.0 84.8 jit_solution(15571798847646412706)
XLA Ops:
  0.0 80.3 %shard_map.55 = (f32[2048,256]{1,0:T(8,128)}, bf16[2048,256]{1,0:T(8,128)(2,1)}, f32[512,256]{1,0:T(8,128)}) custom-call(bf16[16,3,128,128]{3,2,1,0:T(8,128)(2,1)} %ham.1, s32[3,16]{1,0:T(4,128)} %bitcast.1, bf16[2048,2048]{1,0:T(8,128)(2,1)} %phase_l.1, bf16[2048,2048]{1,0:T(8,128)(2,1)} %phase_r.1, bf16[2048,256]{1,0:T(8,128)(2,1)} %o_m.1), custom_call_target="tpu_custom_call" | custom-call | flops 16000000000 | bytes 20971520 | tf_op jit(solution)/shard_map/pallas_call | solution.py:486
  80.4 4.4 %shard_map.56 = f32[2048,256]{1,0:T(8,128)} custom-call(f32[2048,256]{1,0:T(8,128)} %get-tuple-element.8.base, bf16[2048,256]{1,0:T(8,128)(2,1)} %o_m.1, bf16[2048,256]{1,0:T(8,128)(2,1)} %get-tuple-element.9.o_o, f32[512,256]{1,0:T(8,128)} %get-tuple-element.10.cross), custom_call_target="tpu_custom_call" | custom-call | tf_op jit(solution)/shard_map/pallas_call | solution.py:534
